TPU v7x, 32 devices: a whole 2x2x4 slice. The times are simulated.
32 devices in a mesh: front: 4 (over x, core), grp: 8 (over z, y).
Axes of the slice: x: 2, y: 2, z: 4, core: 2. Of those that a mesh axis runs over, the one named last changes fastest.
Arguments:
- contributions: bfloat16 [4096, 16384], P(('front', 'grp')), may hold values from -6 to 6
- sketch_matrix: bfloat16 [16384, 256], P(('front', 'grp')), may hold values from -0.046875 to 0.046875
- destinations: int32 [4096, 1], replicated, may hold values from 0 to 31; in each aligned block of 128 rows (0 to 127, 128 to 255, ...) at most 8 rows name the same one
- parent_rows: int32 [4096], replicated, may hold values from 0 to 1023
- front_sizes: int32 [4], P('front'), may hold values from 4096 to 8192
- leaf_skeleton: int32 [4, 8, 128], P('front', 'grp'), may hold values from 0 to 1023, as said below
- merge_skeleton: int32 [4, 7, 128], P('front'), may hold values from 0 to 255, as said below
Outputs:
- leaf_maps: float32 [4, 8192, 128], P('front', 'grp')
- node_maps: float32 [4, 8, 3, 256, 128], P('front', 'grp')
- top_rows: float32 [4, 8, 128, 256], P('front', 'grp')
Inputs may be any that keep to these rules, and one draw needn't show every extreme that they name: `destinations`: in the rows of one device no destination is named by more than 8 rows. `leaf_skeleton`: each row holds 128 different row numbers of a leaf block. `merge_skeleton`: each row holds 128 different positions of the stacked 2 * 128 rows.
All inputs are finite; a program needn't handle non-finite values.
Results may differ from a plain program's by a relative error of at most 0.003.
Values may be sent and summed in bfloat16 or wider, within the bound.
A program may use at most 64 MiB of HBM per device.

v0:
```python
import jax
import jax.numpy as jnp
from jax import lax
from jax.sharding import PartitionSpec as P

PR_DEV = 1024
LEVELS = 3


def from_partner(block, axis, stride):
    count = lax.axis_size(axis)
    route = []
    for low in range(count):
        high = low | 1 << stride
        if high != low and high < count:
            route += [(low, high), (high, low)]
    return lax.ppermute(block, axis, route)


def ridge_map(rows, basis):
    gram = jnp.dot(basis, basis.T, precision=lax.Precision.HIGHEST)
    shift = 0.1 * jnp.mean(jnp.diagonal(gram)) + 1e-05
    ident = jnp.eye(gram.shape[0], dtype=jnp.float32)
    gram = gram + shift * ident
    approx = ident / jnp.trace(gram)
    for step in range(24):
        approx = jnp.dot(
            approx,
            2.0 * ident - jnp.dot(gram, approx, precision=lax.Precision.HIGHEST),
            precision=lax.Precision.HIGHEST,
        )
    right = jnp.dot(rows, basis.T, precision=lax.Precision.HIGHEST)
    return jnp.dot(right, approx, precision=lax.Precision.HIGHEST)


def select_rows(rows, index):
    picker = (index[:, None] == jnp.arange(rows.shape[0], dtype=jnp.int32)[None, :]).astype(
        jnp.float32
    )
    return jnp.dot(picker, rows, precision=lax.Precision.HIGHEST)


def local(
    contributions,
    sketch_matrix,
    destinations,
    parent_rows,
    front_sizes,
    leaf_skeleton,
    merge_skeleton,
):
    fronts = lax.axis_size("front")
    leaves = lax.axis_size("grp")
    devices = fronts * leaves
    grp_index = lax.axis_index("grp")
    myself = lax.axis_index("front") * leaves + grp_index
    rows_dev = contributions.shape[0]
    width = sketch_matrix.shape[1]
    capacity = 2 * rows_dev // devices
    sketch = jnp.dot(
        contributions,
        lax.all_gather(sketch_matrix, ("front", "grp"), axis=0, tiled=True),
        preferred_element_type=jnp.float32,
    )
    sketch = sketch.astype(jnp.bfloat16)
    every_dest = destinations[:, 0].reshape(devices, rows_dev)
    every_row = parent_rows.reshape(devices, rows_dev)
    mine = lax.dynamic_index_in_dim(every_dest, myself, 0, keepdims=False)
    owners = jnp.arange(devices, dtype=jnp.int32)
    hits = (mine[:, None] == owners[None, :]).astype(jnp.int32)
    before = jnp.cumsum(hits, axis=0) - hits
    slot_of = jnp.sum(before * hits, axis=1)
    keys = mine * capacity + slot_of
    placing = (keys[None, :] == jnp.arange(devices * capacity, dtype=jnp.int32)[:, None]).astype(
        jnp.bfloat16
    )
    packed = jnp.dot(placing, sketch, preferred_element_type=jnp.float32).astype(jnp.bfloat16)
    packed = packed.reshape(devices, capacity, width)
    arrived = lax.all_to_all(
        packed, ("front", "grp"), split_axis=0, concat_axis=0, tiled=True
    ).reshape(devices * capacity, width)
    landing = (every_dest == myself).astype(jnp.int32)
    slots = jnp.cumsum(landing, axis=1) - landing
    match = landing[:, None, :] * (
        slots[:, None, :] == jnp.arange(capacity, dtype=jnp.int32)[None, :, None]
    ).astype(jnp.int32)
    local_row = jnp.sum(match * every_row[:, None, :], axis=2)
    filled = jnp.sum(match, axis=2)
    where_to = jnp.where(filled > 0, local_row, -1).reshape(devices * capacity)
    adding = (jnp.arange(PR_DEV, dtype=jnp.int32)[:, None] == where_to[None, :]).astype(
        jnp.bfloat16
    )
    parent = jnp.dot(adding, arrived, preferred_element_type=jnp.float32)
    global_row = grp_index * PR_DEV + jnp.arange(PR_DEV, dtype=jnp.int32)
    parent = jnp.where((global_row < front_sizes[0])[:, None], parent, jnp.zeros_like(parent))
    basis = select_rows(parent, leaf_skeleton[0, 0])
    leaf_map = ridge_map(parent, basis)
    skeletons = merge_skeleton[0]
    level_maps = []
    current = basis
    for level in range(LEVELS):
        partner = from_partner(current, "grp", level)
        upper_side = grp_index >> level & 1 == 1
        first = jnp.where(upper_side, partner, current)
        second = jnp.where(upper_side, current, partner)
        stacked = jnp.concatenate([first, second], axis=0)
        node = leaves - (leaves >> level) + (grp_index >> level + 1)
        chosen = lax.dynamic_index_in_dim(skeletons, node, 0, keepdims=False)
        current = select_rows(stacked, chosen)
        level_maps.append(ridge_map(stacked, current))
    node_maps = jnp.stack(level_maps, axis=0)
    return (leaf_map[None], node_maps[None, None], current[None, None])


def solution(mesh):
    in_specs = (
        P(("front", "grp"), None),
        P(("front", "grp"), None),
        P(),
        P(),
        P("front"),
        P("front", "grp", None),
        P("front", None, None),
    )
    out_specs = (
        P("front", "grp", None),
        P("front", "grp", None, None, None),
        P("front", "grp", None, None),
    )
    return jax.shard_map(local, mesh=mesh, in_specs=in_specs, out_specs=out_specs, check_vma=False)
```

profile of v0, /device:TPU:0, one launch (start us, length us, event | category | flops | bytes accessed | tf_op | source)
XLA Modules:
  0.0 183.8 jit_solution(14333173300902023975)
XLA Ops:
  7.2 0.7 all-gather.2.cloned.1.call-update
  7.9 0.7 fusion.49
  8.9 0.7 compare_convert_fusion
  9.6 0.3 reduce_window_sum.22
  10.1 0.7 fusion.465
  10.8 1.9 %select_reduce_fusion = (s32[32,8]{1,0:T(8,128)S(1)}, s32[32,8]{1,0:T(8,128)S(1)}) fusion(s32[32,128]{1,0:T(8,128)S(1)} %compare_convert_fusion, s32[32,128]{1,0:T(8,128)S(1)} %fusion.465, s32[32,128]{1,0:T(8,128)} %bitcast.346), kind=kLoop, calls=%fused_computation.124 | loop fusion | flops 163328 | bytes 51200 | tf_op jit(solution)/shard_map/reduce_sum | solution.py:88
  12.7 0.7 fusion.48
  13.4 77.6 %all-gather.2.cloned.1.call-done = bf16[16384,256]{1,0:T(8,128)(2,1)} async-done(((bf16[512,256]{1,0:T(8,128)(2,1)}), bf16[16384,256]{1,0:T(8,128)(2,1)}) %all-gather.2.cloned.1.call-update) | async-done | bytes 8388624 | tf_op jit(solution)/shard_map/all_gather | solution.py:62
  91.0 6.8 %fusion = bf16[32,8,256]{2,1,0:T(8,128)(2,1)} fusion(bf16[128,16384]{1,0:T(8,128)(2,1)} %param.7, bf16[16384,256]{1,0:T(8,128)(2,1)} %all-gather.2.cloned.1.call-done, s32[128]{0:T(128)S(1)} %fusion.48), kind=kOutput, calls=%fused_computation.106 | convolution fusion | flops 1090650112 | bytes 12714496 | tf_op jit(solution)/shard_map/dot_general | solution.py:77
  97.8 3.4 %all-to-all-start = ((bf16[32,8,256]{2,1,0:T(8,128)(2,1)}), bf16[32,8,256]{2,1,0:T(8,128)(2,1)S(1)}, u32[]{:S(2)}, u32[]{:S(2)}) async-start(bf16[32,8,256]{2,1,0:T(8,128)(2,1)} %fusion), calls=%async_computation | async-start | bytes 262144 | tf_op jit(solution)/shard_map/all_to_all | solution.py:79
  101.9 0.7 fusion.45
  102.6 6.1 %all-to-all-done = bf16[32,8,256]{2,1,0:T(8,128)(2,1)S(1)} async-done(((bf16[32,8,256]{2,1,0:T(8,128)(2,1)}), bf16[32,8,256]{2,1,0:T(8,128)(2,1)S(1)}, u32[]{:S(2)}, u32[]{:S(2)}) %all-to-all-start) | async-done | bytes 131104 | tf_op jit(solution)/shard_map/all_to_all | solution.py:79
  108.7 0.3 convolution_select_fusion
  109.0 0.6 fusion.2
  109.6 1.3 collective-permute-start
  110.9 0.3 fusion.65
  111.2 1.0 fusion.64
  112.2 1.2 gather_fusion
  113.4 0.6 reduce_sum.97
  114.7 0.6 select_reduce_fusion.4
  116.0 0.2 select_subtract_fusion.95
  118.1 0.2 select_subtract_fusion.90
  119.4 0.2 select_subtract_fusion.87
  120.3 0.2 select_subtract_fusion.85
  121.5 0.2 select_subtract_fusion.82
  122.8 0.2 select_subtract_fusion.79
  124.9 0.2 select_subtract_fusion.74
  126.2 1.4 convolution_bitcast_fusion
  127.6 0.3 fusion.9
  127.9 0.3 fusion.89
  128.1 0.4 fusion.8
  128.5 0.7 collective-permute-start.1
  129.3 1.5 gather_fusion.1
  130.7 0.6 reduce_sum.99
  132.0 0.6 select_reduce_fusion.3
  133.3 0.2 select_subtract_fusion.71
  134.1 0.2 select_subtract_fusion.69
  140.9 0.2 select_subtract_fusion.53
  141.8 0.2 select_subtract_fusion.51
  143.5 0.3 convolution_bitcast_fusion.3
  143.8 0.3 fusion.7
  144.1 0.3 fusion.113
  144.4 0.4 fusion.6
  144.7 1.3 collective-permute-start.2
  146.1 1.5 gather_fusion.2
  147.6 0.6 reduce_sum.101
  148.8 0.6 select_reduce_fusion.2
  150.2 0.2 select_subtract_fusion.47
  155.7 0.2 select_subtract_fusion.34
  156.5 0.2 select_subtract_fusion.32
  157.4 0.2 select_subtract_fusion.30
  158.2 0.2 select_subtract_fusion.28
  159.1 0.2 select_subtract_fusion.26
  160.4 0.3 convolution_bitcast_fusion.2
  160.7 0.3 fusion.5
  161.0 0.3 fusion.137
  161.2 0.4 fusion.4
  161.6 1.5 gather_fusion.3
  163.2 0.6 reduce_sum.103
  164.4 0.6 select_reduce_fusion.1
  165.7 0.2 select_subtract_fusion.23
  169.6 0.2 select_subtract_fusion.14
  175.9 0.3 convolution_bitcast_fusion.1
  176.2 0.8 maximum_bitcast_fusion
  (191 shorter events, 36.0 us)
Async XLA Ops:
  7.2 101.9 %copy-start.1 = (s32[1,1,128]{2,1,0:T(1,128)S(1)}, s32[1,1,128]{2,1,0:T(1,128)}, u32[]{:S(2)}) copy-start(s32[1,1,128]{2,1,0:T(1,128)} %param.12) | copy-start | bytes 1540
  7.2 83.8 %all-gather.2.cloned.1.call-start = ((), (), s32[]{:S(2)}) async-start(), calls=%async_computation.1 | async-start | bytes 8650752 | tf_op jit(solution)/shard_map/all_gather | solution.py:62
  97.8 10.9 %all-to-all-start = ((bf16[32,8,256]{2,1,0:T(8,128)(2,1)}), bf16[32,8,256]{2,1,0:T(8,128)(2,1)S(1)}, u32[]{:S(2)}, u32[]{:S(2)}) async-start(bf16[32,8,256]{2,1,0:T(8,128)(2,1)} %fusion), calls=%async_computation | async-start | bytes 262144 | tf_op jit(solution)/shard_map/all_to_all | solution.py:79
  109.6 17.9 %collective-permute-start = (f32[128,256]{1,0:T(8,128)S(1)}, f32[128,256]{1,0:T(8,128)S(1)}, u32[]{:S(2)}, u32[]{:S(2)}) collective-permute-start(f32[128,256]{1,0:T(8,128)S(1)} %fusion.2), channel_id=1, source_target_pairs={{0,1},{1,0},{2,3},{3,2},{4,5},{5,4},{6,7},{7,6},{8,9},{9,8},{10,11... | collective-permute-start | bytes 393224 | tf_op jit(solution)/shard_map/ppermute | solution.py:17
  128.5 15.2 %collective-permute-start.1 = (f32[128,256]{1,0:T(8,128)S(1)}, f32[128,256]{1,0:T(8,128)S(1)}, u32[]{:S(2)}, u32[]{:S(2)}) collective-permute-start(f32[128,256]{1,0:T(8,128)S(1)} %fusion.9), channel_id=1, source_target_pairs={{0,2},{2,0},{1,3},{3,1},{4,6},{6,4},{5,7},{7,5},{8,10},{10,8},{9,1... | collective-permute-start | bytes 393224 | tf_op jit(solution)/shard_map/ppermute | solution.py:17
  144.7 15.9 %collective-permute-start.2 = (f32[128,256]{1,0:T(8,128)S(1)}, f32[128,256]{1,0:T(8,128)S(1)}, u32[]{:S(2)}, u32[]{:S(2)}) collective-permute-start(f32[128,256]{1,0:T(8,128)S(1)} %fusion.7), channel_id=1, source_target_pairs={{0,4},{4,0},{1,5},{5,1},{2,6},{6,2},{3,7},{7,3},{8,12},{12,8},{9,1... | collective-permute-start | bytes 393224 | tf_op jit(solution)/shard_map/ppermute | solution.py:17
  160.9 16.0 %copy-start = (f32[128,256]{1,0:T(8,128)}, f32[128,256]{1,0:T(8,128)S(1)}, u32[]{:S(2)}) copy-start(f32[128,256]{1,0:T(8,128)S(1)} %fusion.5) | copy-start | bytes 393220
Sparse Core Ops, SparseCore 0:
  11.0 79.9 all-gather.1
where the time goes:
time: 184 us
  waiting for transfers between devices  84.4 us (46%)
  matrix products  53.1 us (29%)
  between operations  21.9 us (12%)
  other arithmetic  10.5 us (6%)
  local copies, waits for them, and re-layouts  7.25 us (4%)
  starting transfers between devices  6.78 us (4%)
    all_gather x1, waiting for transfers between devices, local(): lax.all_gather(sketch_matrix, ('front', 'grp'), axis=0, tiled=True)  77.6 us
    dot_general x96, matrix products, ridge_map(): jnp.dot(gram, approx, precision=lax.Precision.HIGHEST)  19.7 us
    dot_general x96, matrix products, ridge_map(): jnp.dot(approx, 2.0 * ident - jnp.dot(gram, approx, precision=lax.Precisi...  19.5 us
    dot_general x1, matrix products, local(): jnp.dot(placing, sketch, preferred_element_type=jnp.float32)  6.78 us
    all_to_all x1, waiting for transfers between devices, local(): lax.all_to_all(packed, ('front', 'grp'), split_axis=0, concat_axis=0, til...  6.08 us
    gather x4, local copies, waits for them, and re-layouts, ridge_map(): shift = 0.1 * jnp.mean(jnp.diagonal(gram)) + 1e-05  5.76 us
  transfers between devices with their start and end apart: 5, of which 2 were waited for; matrix products, arithmetic and copies ran while one was open for 25% of the time, Pallas kernels for 0%

commit v1 on v0

v1 whole, which is shorter than its diff:
```python
import functools
import heapq

import jax
import jax.numpy as jnp
from jax import lax
from jax.experimental import pallas as pl
from jax.experimental.pallas import tpu as pltpu
from jax.sharding import PartitionSpec as P

PR_DEV = 1024
LEVELS = 3
STEPS = 24
EXACT_STEPS = 2
HIGHEST = lax.Precision.HIGHEST
MESH = pl.DeviceIdType.MESH


def bits_of(count):
    return count.bit_length() - 1


def flip(value, mask):
    bit = 1
    while bit <= mask:
        if mask & bit:
            value = value + bit * (1 - 2 * lax.rem(lax.div(value, bit), 2))
        bit *= 2
    return value


def exchange_plan(grp_bits, x_bits):
    grp = [1 << b for b in reversed(range(grp_bits))]
    xs = [1 << (grp_bits + b) for b in reversed(range(x_bits))]
    half = grp_bits // 2
    orders = (grp[:1] + xs + grp[1:], grp[:1] + grp[-half:] + grp[1 : len(grp) - half] + xs)
    free = {}
    events = [(0.0, 0, 0), (0.0, 1, 0)]
    sequence = []
    while events:
        now, part, slot = heapq.heappop(events)
        order = orders[part]
        last = max([order.index(d) for d in order if d & slot], default=-1)
        onward = order[last + 1 :]
        sequence.append((part, slot, onward))
        for dim in onward:
            begin = max(now, free.get(dim, 0.0))
            free[dim] = begin + 2.6
            heapq.heappush(events, (begin + 3.6, part, slot ^ dim))
    return sequence


def sketch_kernel(
    fronts, leaves, c_ref, omega_ref, out_ref, cols, slots, acc, partial, local_sem, csend, crecv, send, recv, psem
):
    core = lax.rem(lax.axis_index("front"), 2)
    x_at = lax.div(lax.axis_index("front"), 2)
    grp_at = lax.axis_index("grp")
    x_count = fronts // 2
    grp_bits, x_bits = bits_of(leaves), bits_of(x_count)
    depth = omega_ref.shape[0]
    half = depth // 2
    rows = c_ref.shape[0]
    span = leaves * depth
    sibling = (x_at * 2 + 1 - core, grp_at)

    def partner(dim):
        if dim < leaves:
            return (x_at * 2 + core, flip(grp_at, dim))
        return (flip(x_at, dim // leaves) * 2 + core, grp_at)

    barrier = pltpu.get_barrier_semaphore()
    others = [partner(1 << b) for b in range(grp_bits + x_bits)] + [sibling]
    for other in others:
        pl.semaphore_signal(barrier, inc=1, device_id=other, device_id_type=MESH)
    mine = []
    for x in range(x_count):
        begin = pl.multiple_of((x * 2 + core) * span, 128)
        copy = pltpu.make_async_copy(
            c_ref.at[:, pl.ds(begin, span)], cols.at[0, :, pl.ds(x * span, span)], local_sem.at[x]
        )
        copy.start()
        mine.append(copy)
    pl.semaphore_wait(barrier, len(others))

    def piece(ref, part):
        return ref.at[pl.ds(part * half, half), :]

    def start(part, slot, dim):
        source = omega_ref if slot == 0 else slots.at[slot]
        copy = pltpu.make_async_remote_copy(
            src_ref=piece(source, part),
            dst_ref=piece(slots.at[slot ^ dim], part),
            send_sem=send.at[part, slot ^ dim],
            recv_sem=recv.at[part, slot ^ dim],
            device_id=partner(dim),
            device_id_type=MESH,
        )
        copy.start()
        return copy

    sequence = exchange_plan(grp_bits, x_bits)
    arrivals = {}
    given = []
    for part, slot, onward in sequence:
        if slot == 0:
            for dim in onward:
                arrivals[part, dim] = start(part, slot, dim)
    for x in range(x_count):
        begin = pl.multiple_of((x * 2 + 1 - core) * span, 128)
        copy = pltpu.make_async_remote_copy(
            src_ref=c_ref.at[:, pl.ds(begin, span)],
            dst_ref=cols.at[1, :, pl.ds(x * span, span)],
            send_sem=csend.at[x],
            recv_sem=crecv.at[x],
            device_id=sibling,
            device_id_type=MESH,
        )
        copy.start()
        given.append(copy)

    acc[...] = jnp.zeros_like(acc)
    ready = False
    waiting = []

    def multiply(part, slot):
        x_from = flip(x_at, slot // leaves)
        grp_from = flip(grp_at, slot % leaves)
        begin = pl.multiple_of((x_from * leaves + grp_from) * depth + part * half, 128)
        left = cols[:, :, pl.ds(begin, half)].reshape(2 * rows, half)
        source = omega_ref if slot == 0 else slots.at[slot]
        right = source[pl.ds(part * half, half), :]
        acc[...] += jnp.dot(left, right, preferred_element_type=jnp.float32)

    for number, (part, slot, onward) in enumerate(sequence):
        if slot != 0:
            arrivals[part, slot].wait_recv()
            for dim in onward:
                arrivals[part, slot ^ dim] = start(part, slot, dim)
        waiting.append((part, slot))
        if number >= 6 or number == len(sequence) - 1:
            if not ready:
                for copy in mine:
                    copy.wait()
                for copy in given:
                    copy.wait_recv()
                ready = True
            for item in waiting:
                multiply(*item)
            waiting = []

    final = pltpu.make_async_remote_copy(
        src_ref=acc.at[pl.ds(rows, rows), :],
        dst_ref=partial,
        send_sem=psem.at[0],
        recv_sem=psem.at[1],
        device_id=sibling,
        device_id_type=MESH,
    )
    final.start()
    for copy in given:
        copy.wait_send()
    for copy in arrivals.values():
        copy.wait_send()
    final.wait()
    out_ref[...] = (acc[pl.ds(0, rows), :] + partial[...]).astype(out_ref.dtype)


def make_sketch(contributions, omega):
    fronts, leaves = lax.axis_size("front"), lax.axis_size("grp")
    rows, order = contributions.shape
    depth, width = omega.shape
    count = fronts * leaves // 2
    return pl.pallas_call(
        functools.partial(sketch_kernel, fronts, leaves),
        out_shape=jax.ShapeDtypeStruct((rows, width), jnp.bfloat16),
        in_specs=[pl.BlockSpec(memory_space=pl.ANY), pl.BlockSpec(memory_space=pltpu.VMEM)],
        out_specs=pl.BlockSpec(memory_space=pltpu.VMEM),
        scratch_shapes=[
            pltpu.VMEM((2, rows, order // 2), jnp.bfloat16),
            pltpu.VMEM((count, depth, width), jnp.bfloat16),
            pltpu.VMEM((2 * rows, width), jnp.float32),
            pltpu.VMEM((rows, width), jnp.float32),
            pltpu.SemaphoreType.DMA((fronts // 2,)),
            pltpu.SemaphoreType.DMA((fronts // 2,)),
            pltpu.SemaphoreType.DMA((fronts // 2,)),
            pltpu.SemaphoreType.DMA((2, count)),
            pltpu.SemaphoreType.DMA((2, count)),
            pltpu.SemaphoreType.DMA((2,)),
        ],
        compiler_params=pltpu.CompilerParams(
            collective_id=0, has_side_effects=True, vmem_limit_bytes=40 * 2**20
        ),
        cost_estimate=pl.CostEstimate(
            flops=2 * rows * order * width, bytes_accessed=2 * rows * order, transcendentals=0
        ),
    )(contributions, omega)


def split(value):
    high = value.astype(jnp.bfloat16)
    return high, (value - high.astype(jnp.float32)).astype(jnp.bfloat16)


def halves(value):
    width = value.shape[1] // 2
    return value[:, :width] + value[:, width:]


def split_dot(left, right):
    lh, ll = split(left)
    rh, rl = split(right)
    both = jnp.concatenate([lh, ll], axis=1)
    top = jnp.concatenate([rh, rl], axis=1)
    low = jnp.concatenate([rh, jnp.zeros_like(rl)], axis=1)
    weights = jnp.concatenate([top, low], axis=0)
    return halves(jnp.dot(both, weights, preferred_element_type=jnp.float32))


def solve_kernel(arrived_ref, where_ref, basis_ref, stack_refs, pick_refs, leaf_ref, node_ref, state, gram_ref):
    bases = [basis_ref] + list(pick_refs)
    rank = basis_ref.shape[0]
    row = lax.broadcasted_iota(jnp.int32, (rank, rank), 0)
    col = lax.broadcasted_iota(jnp.int32, (rank, rank), 1)
    ident = (row == col).astype(jnp.float32)
    for at, ref in enumerate(bases):
        basis = ref[...]
        gram = lax.dot_general(
            basis, basis, (((1,), (1,)), ((), ())), precision=HIGHEST, preferred_element_type=jnp.float32
        )
        shift = 0.1 * (jnp.sum(gram * ident, keepdims=True) / rank) + 1e-05
        gram = gram + shift * ident
        scale = 1.0 / jnp.sum(gram * ident, keepdims=True)
        gram_ref[at] = gram
        rest = ident - gram * scale
        state[at, pl.ds(0, rank), :] = (ident + rest) * scale
        state[at, pl.ds(rank, rank), :] = split_dot(rest, rest)

    def step(_, carry):
        for at in range(len(bases)):
            now = state[at]
            grown = split_dot(now, now[rank:])
            state[at, pl.ds(0, rank), :] = now[:rank] + grown[:rank]
            state[at, pl.ds(rank, rank), :] = grown[rank:]
        return carry

    lax.fori_loop(0, STEPS - EXACT_STEPS - 1, step, 0)
    approx = [state[at, pl.ds(0, rank), :] for at in range(len(bases))]
    for _ in range(EXACT_STEPS):
        inner = [
            2.0 * ident - jnp.dot(gram_ref[at], approx[at], precision=HIGHEST, preferred_element_type=jnp.float32)
            for at in range(len(bases))
        ]
        approx = [
            jnp.dot(approx[at], inner[at], precision=HIGHEST, preferred_element_type=jnp.float32)
            for at in range(len(bases))
        ]
    lifted = [
        jnp.dot(jnp.transpose(ref[...]), approx[at], precision=HIGHEST, preferred_element_type=jnp.float32)
        for at, ref in enumerate(bases)
    ]
    spread = jnp.concatenate(split(lifted[0]), axis=1)
    small = halves(jnp.dot(arrived_ref[...], spread, preferred_element_type=jnp.float32))
    small = jnp.concatenate(split(small), axis=1)
    slots = arrived_ref.shape[0]
    adding = (
        lax.broadcasted_iota(jnp.int32, (leaf_ref.shape[0], slots), 0) == where_ref[...]
    ).astype(jnp.float32).astype(jnp.bfloat16)
    leaf_ref[...] = halves(jnp.dot(adding, small, preferred_element_type=jnp.float32))
    for level, ref in enumerate(stack_refs):
        node_ref[level] = split_dot(ref[...], lifted[level + 1])


def solve_all(arrived, where_to, basis, stacks, picks):
    rank = basis.shape[0]
    vmem = pl.BlockSpec(memory_space=pltpu.VMEM)
    levels = len(stacks)
    return pl.pallas_call(
        solve_kernel,
        out_shape=(
            jax.ShapeDtypeStruct((PR_DEV, rank), jnp.float32),
            jax.ShapeDtypeStruct((levels, 2 * rank, rank), jnp.float32),
        ),
        in_specs=[vmem, vmem, vmem, [vmem] * levels, [vmem] * levels],
        out_specs=(vmem, vmem),
        scratch_shapes=[
            pltpu.VMEM((levels + 1, 2 * rank, rank), jnp.float32),
            pltpu.VMEM((levels + 1, rank, rank), jnp.float32),
        ],
        compiler_params=pltpu.CompilerParams(vmem_limit_bytes=40 * 2**20),
    )(arrived, where_to, basis, stacks, picks)


def from_partner(block, axis, stride):
    count = lax.axis_size(axis)
    route = []
    for low in range(count):
        high = low | 1 << stride
        if high != low and high < count:
            route += [(low, high), (high, low)]
    return lax.ppermute(block, axis, route)


def select_rows(rows, index):
    picker = (index[:, None] == jnp.arange(rows.shape[0], dtype=jnp.int32)[None, :]).astype(
        jnp.float32
    )
    return jnp.dot(picker, rows, precision=HIGHEST)


def local(
    contributions,
    sketch_matrix,
    destinations,
    parent_rows,
    front_sizes,
    leaf_skeleton,
    merge_skeleton,
):
    fronts = lax.axis_size("front")
    leaves = lax.axis_size("grp")
    devices = fronts * leaves
    grp_index = lax.axis_index("grp")
    myself = lax.axis_index("front") * leaves + grp_index
    rows_dev = contributions.shape[0]
    width = sketch_matrix.shape[1]
    capacity = 2 * rows_dev // devices
    sketch = make_sketch(contributions, sketch_matrix)
    every_dest = destinations[:, 0].reshape(devices, rows_dev)
    every_row = parent_rows.reshape(devices, rows_dev)
    mine = lax.dynamic_index_in_dim(every_dest, myself, 0, keepdims=False)
    owners = jnp.arange(devices, dtype=jnp.int32)
    hits = (mine[:, None] == owners[None, :]).astype(jnp.int32)
    before = jnp.cumsum(hits, axis=0) - hits
    slot_of = jnp.sum(before * hits, axis=1)
    keys = mine * capacity + slot_of
    placing = (keys[None, :] == jnp.arange(devices * capacity, dtype=jnp.int32)[:, None]).astype(
        jnp.bfloat16
    )
    packed = jnp.dot(placing, sketch, preferred_element_type=jnp.float32).astype(jnp.bfloat16)
    packed = packed.reshape(devices, capacity, width)
    arrived = lax.all_to_all(
        packed, ("front", "grp"), split_axis=0, concat_axis=0, tiled=True
    ).reshape(devices * capacity, width)
    landing = (every_dest == myself).astype(jnp.int32)
    slots = jnp.cumsum(landing, axis=1) - landing
    match = landing[:, None, :] * (
        slots[:, None, :] == jnp.arange(capacity, dtype=jnp.int32)[None, :, None]
    ).astype(jnp.int32)
    local_row = jnp.sum(match * every_row[:, None, :], axis=2)
    filled = jnp.sum(match, axis=2)
    live = (filled > 0) & (grp_index * PR_DEV + local_row < front_sizes[0])
    where_to = jnp.where(live, local_row, -1).reshape(1, devices * capacity)
    chosen = (leaf_skeleton[0, 0][:, None] == where_to).astype(jnp.bfloat16)
    basis = jnp.dot(chosen, arrived, preferred_element_type=jnp.float32)
    skeletons = merge_skeleton[0]
    stacks, picks = [], []
    current = basis
    for level in range(LEVELS):
        partner = from_partner(current, "grp", level)
        upper_side = grp_index >> level & 1 == 1
        first = jnp.where(upper_side, partner, current)
        second = jnp.where(upper_side, current, partner)
        stacked = jnp.concatenate([first, second], axis=0)
        node = leaves - (leaves >> level) + (grp_index >> level + 1)
        index = lax.dynamic_index_in_dim(skeletons, node, 0, keepdims=False)
        current = select_rows(stacked, index)
        stacks.append(stacked)
        picks.append(current)
    leaf_map, node_maps = solve_all(arrived, where_to, basis, stacks, picks)
    return (leaf_map[None], node_maps[None, None], current[None, None])


def solution(mesh):
    in_specs = (
        P(("front", "grp"), None),
        P(("front", "grp"), None),
        P(),
        P(),
        P("front"),
        P("front", "grp", None),
        P("front", None, None),
    )
    out_specs = (
        P("front", "grp", None),
        P("front", "grp", None, None, None),
        P("front", "grp", None, None),
    )
    return jax.shard_map(local, mesh=mesh, in_specs=in_specs, out_specs=out_specs, check_vma=False)
```

time: 184 us -> 89.6 us (0.49)
  waiting for transfers between devices: 84.4 us -> 19 us
  Pallas kernels: 0 us -> 53.3 us
  matrix products: 53.1 us -> 1.84 us
  between operations: 21.9 us -> 1.47 us
  other arithmetic: 10.5 us -> 2.72 us
  local copies, waits for them, and re-layouts: 7.25 us -> 4.95 us
    all_gather x1 -> x0, waiting for transfers between devices: 77.6 us -> none  [local(): lax.all_gather(sketch_matrix, ('front', 'grp'), axis=0, tiled=True)]
    pallas_call x0 -> x2, Pallas kernels: none -> 53.3 us  [the longest x1 41.1 us: make_sketch(): pl.pallas_call(functools.partial(sketch_kernel, fronts, leaves), out_shap...]
    dot_general x209 -> x4, matrix products: 46.3 us -> 1.01 us  [the longest x3 0.8 us: select_rows(): return jnp.dot(picker, rows, precision=HIGHEST)]
    ppermute x3, waiting for transfers between devices: 0.01 us -> 13.6 us  [from_partner(): return lax.ppermute(block, axis, route)]
    dot_general x1, matrix products: 6.78 us -> 0.83 us  [local(): jnp.dot(placing, sketch, preferred_element_type=jnp.float32)]
    gather x4 -> x0, local copies, waits for them, and re-layouts: 5.76 us -> none  [ridge_map(): shift = 0.1 * jnp.mean(jnp.diagonal(gram)) + 1e-05]
    reduce_sum x8 -> x0, other arithmetic: 4.88 us -> none  [the longest x4 2.48 us: ridge_map(): approx = ident / jnp.trace(gram)]
    unnamed x4 -> x12, local copies, waits for them, and re-layouts: 0.01 us -> 3.16 us
  transfers between devices with their start and end apart: 5 -> 4, of which waited for: 2 -> 4; matrix products, arithmetic and copies ran while one was open for 25% -> 3% of each run, Pallas kernels for 0% -> 0%
where the time goes in v1:
time: 89.6 us; the launch traced here: 89.3 us
  Pallas kernels  53.3 us (59%)
  waiting for transfers between devices  19 us (21%)
  starting transfers between devices  5.94 us (7%)
  local copies, waits for them, and re-layouts  4.95 us (6%)
  other arithmetic  2.72 us (3%)
  matrix products  1.84 us (2%)
  between operations  1.47 us (2%)
    pallas_call x1, Pallas kernels, make_sketch(): pl.pallas_call(functools.partial(sketch_kernel, fronts, leaves), out_shap...  41.1 us
    ppermute x3, waiting for transfers between devices, from_partner(): return lax.ppermute(block, axis, route)  13.6 us
    pallas_call x1, Pallas kernels, solve_all(): pl.pallas_call(solve_kernel, out_shape=(jax.ShapeDtypeStruct((PR_DEV, ran...  12.2 us
    all_to_all x1, waiting for transfers between devices, local(): lax.all_to_all(packed, ('front', 'grp'), split_axis=0, concat_axis=0, til...  5.39 us
    ppermute x3, starting transfers between devices, from_partner(): return lax.ppermute(block, axis, route)  3.36 us
    unnamed x12, local copies, waits for them, and re-layouts  3.16 us
    all_to_all x1, starting transfers between devices, local(): lax.all_to_all(packed, ('front', 'grp'), split_axis=0, concat_axis=0, til...  2.58 us
  transfers between devices with their start and end apart: 4, of which 4 were waited for; matrix products, arithmetic and copies ran while one was open for 3% of the time, Pallas kernels for 0%

profile of v1, /device:TPU:0, one launch (start us, length us, event | category | flops | bytes accessed | tf_op | source)
XLA Modules:
  0.0 89.3 jit_solution(10454339054064660916)
XLA Ops:
  0.6 0.0 copy-start.3
  0.6 0.0 copy-start.4
  0.7 0.0 copy-start.5
  0.7 0.7 fusion.18
  1.4 0.1 fusion.12
  1.5 0.2 reduce_window_sum.22
  1.7 0.2 select_reduce_fusion.1
  1.8 0.7 fusion.17
  2.5 0.0 copy-start
  2.5 2.2 %copy-done = bf16[128,16384]{1,0:T(8,128)(2,1)S(1)} copy-done((bf16[128,16384]{1,0:T(8,128)(2,1)S(1)}, bf16[128,16384]{1,0:T(8,128)(2,1)}, u32[]{:S(2)}) %copy-start) | copy-done | bytes 4194328
  4.7 0.0 copy-start.2
  4.7 0.9 %copy-done.2 = bf16[512,256]{1,0:T(8,128)(2,1)S(1)} copy-done((bf16[512,256]{1,0:T(8,128)(2,1)S(1)}, bf16[512,256]{1,0:T(8,128)(2,1)}, u32[]{:S(2)}) %copy-start.2) | copy-done | bytes 262168
  5.7 41.1 %shard_map.94 = bf16[128,256]{1,0:T(8,128)(2,1)S(1)} custom-call(bf16[128,16384]{1,0:T(8,128)(2,1)S(1)} %copy-done, bf16[512,256]{1,0:T(8,128)(2,1)S(1)} %copy-done.2), custom_call_target="tpu_custom_call" | custom-call | flops 1073741824 | bytes 4194304 | tf_op jit(solution)/shard_map/pallas_call | solution.py:174
  46.8 0.8 fusion
  47.6 2.6 %all-to-all-start = ((bf16[32,8,256]{2,1,0:T(8,128)(2,1)}), bf16[32,8,256]{2,1,0:T(8,128)(2,1)S(1)}, u32[]{:S(2)}, u32[]{:S(2)}) async-start(bf16[32,8,256]{2,1,0:T(8,128)(2,1)} %fusion), calls=%async_computation | async-start | bytes 262144 | tf_op jit(solution)/shard_map/all_to_all | solution.py:342
  50.2 0.0 copy-done.3
  50.3 0.3 reduce_window_sum.23
  50.5 0.0 copy-done.4
  50.6 1.2 %select_reduce_fusion = (s32[32,8]{1,0:T(8,128)S(1)}, s32[32,8]{1,0:T(8,128)S(1)}) fusion(s32[32,128]{1,0:T(8,128)S(1)} %compare_convert_fusion, s32[32,128]{1,0:T(8,128)S(1)} %fusion.21, s32[32,128]{1,0:T(8,128)S(1)} %bitcast.35), kind=kLoop, calls=%fused_computation.6 | loop fusion | flops 163328 | bytes 51200 | tf_op jit(solution)/shard_map/reduce_sum | solution.py:351
  52.4 0.1 gt.23
  52.5 0.1 reduce_sum.38
  52.6 5.4 %all-to-all-done = bf16[32,8,256]{2,1,0:T(8,128)(2,1)S(1)} async-done(((bf16[32,8,256]{2,1,0:T(8,128)(2,1)}), bf16[32,8,256]{2,1,0:T(8,128)(2,1)S(1)}, u32[]{:S(2)}, u32[]{:S(2)}) %all-to-all-start) | async-done | bytes 131104 | tf_op jit(solution)/shard_map/all_to_all | solution.py:342
  58.0 0.0 copy-done.5
  58.0 0.2 fusion.5.basis_ref
  58.2 1.3 %collective-permute-start = (f32[128,256]{1,0:T(8,128)S(1)}, f32[128,256]{1,0:T(8,128)S(1)}, u32[]{:S(2)}, u32[]{:S(2)}) collective-permute-start(f32[128,256]{1,0:T(8,128)S(1)} %fusion.5.basis_ref), channel_id=1, source_target_pairs={{0,1},{1,0},{2,3},{3,2},{4,5},{5,4},{6,7},{7,6},{8,9},{9,8},{10,11... | collective-permute-start | bytes 393224 | tf_op jit(solution)/shard_map/ppermute | solution.py:301
  59.5 0.1 gt.22
  59.6 0.1 reduce_sum.37
  59.7 0.7 fusion.14
  60.4 3.4 %collective-permute-done = f32[128,256]{1,0:T(8,128)S(1)} collective-permute-done((f32[128,256]{1,0:T(8,128)S(1)}, f32[128,256]{1,0:T(8,128)S(1)}, u32[]{:S(2)}, u32[]{:S(2)}) %collective-permute-start) | collective-permute-done | bytes 131104 | tf_op jit(solution)/shard_map/ppermute | solution.py:301
  63.8 0.3 fusion.2.pick_refs_0_
  64.1 0.6 collective-permute-start.1
  64.7 4.4 %collective-permute-done.1 = f32[128,256]{1,0:T(8,128)S(1)} collective-permute-done((f32[128,256]{1,0:T(8,128)S(1)}, f32[128,256]{1,0:T(8,128)S(1)}, u32[]{:S(2)}, u32[]{:S(2)}) %collective-permute-start.1) | collective-permute-done | bytes 131104 | tf_op jit(solution)/shard_map/ppermute | solution.py:301
  69.1 0.3 fusion.3.pick_refs_1_
  69.4 1.4 %collective-permute-start.2 = (f32[128,256]{1,0:T(8,128)S(1)}, f32[128,256]{1,0:T(8,128)S(1)}, u32[]{:S(2)}, u32[]{:S(2)}) collective-permute-start(f32[128,256]{1,0:T(8,128)S(1)} %fusion.3.pick_refs_1_), channel_id=1, source_target_pairs={{0,4},{4,0},{1,5},{5,1},{2,6},{6,2},{3,7},{7,3},{8,12},{12,8},{9,1... | collective-permute-start | bytes 393224 | tf_op jit(solution)/shard_map/ppermute | solution.py:301
  70.9 5.9 %collective-permute-done.2 = f32[128,256]{1,0:T(8,128)S(1)} collective-permute-done((f32[128,256]{1,0:T(8,128)S(1)}, f32[128,256]{1,0:T(8,128)S(1)}, u32[]{:S(2)}, u32[]{:S(2)}) %collective-permute-start.2) | collective-permute-done | bytes 131104 | tf_op jit(solution)/shard_map/ppermute | solution.py:301
  76.8 0.3 fusion.4.pick_refs_2_
  77.1 0.0 copy-start.1
  77.1 12.2 %shard_map.95 = (f32[1024,128]{1,0:T(8,128)}, f32[3,256,128]{2,1,0:T(8,128)}) custom-call(bf16[256,256]{1,0:T(8,128)(2,1)S(1)} %bitcast.29, s32[1,256]{1,0:T(1,128)S(1)} %and_select_fusion.where_ref, f32[128,256]{1,0:T(8,128)S(1)} %fusion.5.basis_ref, f32[256,256]{1,0:T(8,128)S(1)} %pad_maximum_fusion.stack_refs_0_, ...), custom_call_target="tpu_custom_call" | custom-call | tf_op jit(solution)/shard_map/pallas_call | solution.py:278
  89.3 0.0 copy-done.1
  (11 shorter events, 0.2 us)
Async XLA Ops:
  0.6 49.6 %copy-start.3 = (s32[4096,1]{0,1:T(1,128)S(1)}, s32[4096,1]{0,1:T(1,128)}, u32[]{:S(2)}) copy-start(s32[4096,1]{0,1:T(1,128)} %param.9) | copy-start | bytes 49156
  0.6 49.9 %copy-start.4 = (s32[4096]{0:T(1024)S(1)}, s32[4096]{0:T(1024)}, u32[]{:S(2)}) copy-start(s32[4096]{0:T(1024)} %param.10) | copy-start | bytes 49156
  0.7 57.3 %copy-start.5 = (s32[1,1,128]{2,1,0:T(1,128)S(1)}, s32[1,1,128]{2,1,0:T(1,128)}, u32[]{:S(2)}) copy-start(s32[1,1,128]{2,1,0:T(1,128)} %param.12) | copy-start | bytes 1540
  2.5 2.2 %copy-start = (bf16[128,16384]{1,0:T(8,128)(2,1)S(1)}, bf16[128,16384]{1,0:T(8,128)(2,1)}, u32[]{:S(2)}) copy-start(bf16[128,16384]{1,0:T(8,128)(2,1)} %c_ref.1) | copy-start | bytes 12582916
  4.7 0.9 %copy-start.2 = (bf16[512,256]{1,0:T(8,128)(2,1)S(1)}, bf16[512,256]{1,0:T(8,128)(2,1)}, u32[]{:S(2)}) copy-start(bf16[512,256]{1,0:T(8,128)(2,1)} %omega_ref.1) | copy-start | bytes 786436
  47.6 10.3 %all-to-all-start = ((bf16[32,8,256]{2,1,0:T(8,128)(2,1)}), bf16[32,8,256]{2,1,0:T(8,128)(2,1)S(1)}, u32[]{:S(2)}, u32[]{:S(2)}) async-start(bf16[32,8,256]{2,1,0:T(8,128)(2,1)} %fusion), calls=%async_computation | async-start | bytes 262144 | tf_op jit(solution)/shard_map/all_to_all | solution.py:342
  58.2 5.6 %collective-permute-start = (f32[128,256]{1,0:T(8,128)S(1)}, f32[128,256]{1,0:T(8,128)S(1)}, u32[]{:S(2)}, u32[]{:S(2)}) collective-permute-start(f32[128,256]{1,0:T(8,128)S(1)} %fusion.5.basis_ref), channel_id=1, source_target_pairs={{0,1},{1,0},{2,3},{3,2},{4,5},{5,4},{6,7},{7,6},{8,9},{9,8},{10,11... | collective-permute-start | bytes 393224 | tf_op jit(solution)/shard_map/ppermute | solution.py:301
  64.1 5.0 %collective-permute-start.1 = (f32[128,256]{1,0:T(8,128)S(1)}, f32[128,256]{1,0:T(8,128)S(1)}, u32[]{:S(2)}, u32[]{:S(2)}) collective-permute-start(f32[128,256]{1,0:T(8,128)S(1)} %fusion.2.pick_refs_0_), channel_id=1, source_target_pairs={{0,2},{2,0},{1,3},{3,1},{4,6},{6,4},{5,7},{7,5},{8,10},{10,8},{9,1... | collective-permute-start | bytes 393224 | tf_op jit(solution)/shard_map/ppermute | solution.py:301
  69.4 7.3 %collective-permute-start.2 = (f32[128,256]{1,0:T(8,128)S(1)}, f32[128,256]{1,0:T(8,128)S(1)}, u32[]{:S(2)}, u32[]{:S(2)}) collective-permute-start(f32[128,256]{1,0:T(8,128)S(1)} %fusion.3.pick_refs_1_), channel_id=1, source_target_pairs={{0,4},{4,0},{1,5},{5,1},{2,6},{6,2},{3,7},{7,3},{8,12},{12,8},{9,1... | collective-permute-start | bytes 393224 | tf_op jit(solution)/shard_map/ppermute | solution.py:301
  77.1 12.2 %copy-start.1 = (f32[128,256]{1,0:T(8,128)}, f32[128,256]{1,0:T(8,128)S(1)}, u32[]{:S(2)}) copy-start(f32[128,256]{1,0:T(8,128)S(1)} %fusion.4.pick_refs_2_) | copy-start | bytes 393220

commit v2 on v0

v2 whole, which is shorter than its diff:
```python
import functools
import heapq

import jax
import jax.numpy as jnp
from jax import lax
from jax.experimental import pallas as pl
from jax.experimental.pallas import tpu as pltpu
from jax.sharding import PartitionSpec as P

PR_DEV = 1024
LEVELS = 3
STEPS = 24
EXACT_STEPS = 2
CUTS = 4
HIGHEST = lax.Precision.HIGHEST
MESH = pl.DeviceIdType.MESH


def bits_of(count):
    return count.bit_length() - 1


def flip(value, mask):
    bit = 1
    while bit <= mask:
        if mask & bit:
            value = value + bit * (1 - 2 * lax.rem(lax.div(value, bit), 2))
        bit *= 2
    return value


def exchange_plan(grp_bits, x_bits, cuts):
    grp = [1 << b for b in reversed(range(grp_bits))]
    xs = [1 << (grp_bits + b) for b in reversed(range(x_bits))]
    half = grp_bits // 2
    near = grp[-half:]
    orders = (grp[:1] + xs + grp[1:], grp[:1] + near + grp[1 : len(grp) - half] + xs)
    link = {d: "x" if d in xs else "near" if d in near else "far" for d in grp + xs}
    free = {}
    events = [(0.0, part, 0) for part in range(cuts)]
    sequence = []
    while events:
        now, part, slot = heapq.heappop(events)
        order = orders[part % 2]
        last = max([order.index(d) for d in order if d & slot], default=-1)
        onward = order[last + 1 :]
        sequence.append((part, slot, onward))
        for dim in onward:
            begin = max(now, free.get(link[dim], 0.0))
            free[link[dim]] = begin + 1.0
            heapq.heappush(events, (begin + 1.0 + 0.2 * cuts, part, slot ^ dim))
    return sequence


def split(value):
    high = value.astype(jnp.bfloat16)
    return high, (value - high.astype(jnp.float32)).astype(jnp.bfloat16)


def halves(value):
    width = value.shape[1] // 2
    return value[:, :width] + value[:, width:]


def split_dot(left, right):
    lh, ll = split(left)
    rh, rl = split(right)
    both = jnp.concatenate([lh, ll], axis=1)
    top = jnp.concatenate([rh, rl], axis=1)
    low = jnp.concatenate([rh, jnp.zeros_like(rl)], axis=1)
    weights = jnp.concatenate([top, low], axis=0)
    return halves(jnp.dot(both, weights, preferred_element_type=jnp.float32))


def full_dot(left, right):
    return jnp.dot(left, right, precision=HIGHEST, preferred_element_type=jnp.float32)


def take_rows(picker, rows):
    width = rows.shape[1]
    high, rest = split(rows)
    rest = rows - high.astype(jnp.float32)
    middle, low = split(rest)
    parts = jnp.concatenate([high, middle, low], axis=1)
    found = jnp.dot(picker, parts, preferred_element_type=jnp.float32)
    return (found[:, :width] + found[:, width : 2 * width]) + found[:, 2 * width :]


def as_bf16(condition):
    return condition.astype(jnp.float32).astype(jnp.bfloat16)


def column_of(line):
    return jnp.transpose(jnp.broadcast_to(line.astype(jnp.float32), (128, line.shape[1])))


def whole_kernel(
    fronts, leaves, capacity,
    c_ref, omega_ref, dest_ref, prow_ref, size_ref, leafskel_ref, mergeskel_ref,
    leaf_ref, node_ref, top_ref,
    cols, slots, acc, partial, packed, arrived, stacks, bases, grams, state,
    local_sem, csend, crecv, send, recv, psem, asend, arecv, lsend, lrecv,
):
    front_at = lax.axis_index("front")
    grp_at = lax.axis_index("grp")
    core = lax.rem(front_at, 2)
    x_at = lax.div(front_at, 2)
    devices = fronts * leaves
    myself = front_at * leaves + grp_at
    x_count = fronts // 2
    grp_bits, x_bits = bits_of(leaves), bits_of(x_count)
    depth = omega_ref.shape[0]
    cut = depth // CUTS
    rows, width = c_ref.shape[0], omega_ref.shape[1]
    span = leaves * depth
    rank = leafskel_ref.shape[1]
    sibling = (x_at * 2 + 1 - core, grp_at)

    def device(number):
        return (lax.div(number, leaves), lax.rem(number, leaves))

    def partner(dim):
        if dim < leaves:
            return (front_at, flip(grp_at, dim))
        return (flip(x_at, dim // leaves) * 2 + core, grp_at)

    barrier = pltpu.get_barrier_semaphore()

    def greet(step, carry):
        other = device(lax.rem(myself + step, devices))
        pl.semaphore_signal(barrier, inc=1, device_id=other, device_id_type=MESH)
        return carry

    lax.fori_loop(1, devices, greet, 0)
    mine = []
    for x in range(x_count):
        begin = pl.multiple_of((x * 2 + core) * span, 128)
        copy = pltpu.make_async_copy(
            c_ref.at[:, pl.ds(begin, span)], cols.at[0, :, pl.ds(x * span, span)], local_sem.at[x]
        )
        copy.start()
        mine.append(copy)
    pl.semaphore_wait(barrier, devices - 1)

    def start(part, slot, dim):
        source = omega_ref if slot == 0 else slots.at[slot]
        copy = pltpu.make_async_remote_copy(
            src_ref=source.at[pl.ds(part * cut, cut), :],
            dst_ref=slots.at[slot ^ dim, pl.ds(part * cut, cut), :],
            send_sem=send.at[part, slot ^ dim],
            recv_sem=recv.at[part, slot ^ dim],
            device_id=partner(dim),
            device_id_type=MESH,
        )
        copy.start()
        return copy

    sequence = exchange_plan(grp_bits, x_bits, CUTS)
    arrivals = {}
    given = []
    for part, slot, onward in sequence:
        if slot == 0:
            for dim in onward:
                arrivals[part, dim] = start(part, slot, dim)
    for x in range(x_count):
        begin = pl.multiple_of((x * 2 + 1 - core) * span, 128)
        copy = pltpu.make_async_remote_copy(
            src_ref=c_ref.at[:, pl.ds(begin, span)],
            dst_ref=cols.at[1, :, pl.ds(x * span, span)],
            send_sem=csend.at[x],
            recv_sem=crecv.at[x],
            device_id=sibling,
            device_id_type=MESH,
        )
        copy.start()
        given.append(copy)

    acc[...] = jnp.zeros_like(acc)

    chunks = width // 128
    used = capacity * chunks
    lines = packed.shape[1]
    shape = (devices, lines, rows)
    block_at = lax.broadcasted_iota(jnp.int32, shape, 0).astype(jnp.float32)
    line_at = lax.broadcasted_iota(jnp.int32, shape, 1)
    slot_at = jnp.where(line_at < used, lax.rem(line_at, capacity), -1).astype(jnp.float32)
    row = lax.broadcasted_iota(jnp.int32, (rows, rows), 0)
    col = lax.broadcasted_iota(jnp.int32, (rows, rows), 1)
    going = dest_ref[pl.ds(myself, 1), :].astype(jnp.float32)
    same = (column_of(going)[:, :rows] == going) & (row < col)
    rank_in = jnp.sum(same.astype(jnp.float32), axis=0, keepdims=True)
    placing = as_bf16((block_at == going.reshape(1, 1, rows)) & (slot_at == rank_in.reshape(1, 1, rows)))
    placing = placing.reshape(devices * lines, rows)

    coming = dest_ref[...] == myself
    ahead = jnp.dot(as_bf16(coming), as_bf16(row < col), preferred_element_type=jnp.float32)
    ahead = jnp.where(coming, ahead, -2.0)
    live = prow_ref[...] + grp_at * PR_DEV < size_ref[...]
    landing = jnp.where(live, prow_ref[...] + 1, 0).astype(jnp.float32)
    hit = ahead.reshape(devices, 1, rows) == slot_at
    where_to = jnp.sum(jnp.where(hit, landing.reshape(devices, 1, rows), 0.0), axis=2, keepdims=True) - 1.0
    where_to = where_to.reshape(devices * lines, 1)
    where_to = jnp.transpose(jnp.broadcast_to(where_to, (devices * lines, 128)))[0:1, :]
    chosen = as_bf16(column_of(leafskel_ref[...])[:, 0:1] == where_to)
    picks = []
    for level in range(LEVELS):
        node = leaves - leaves // 2**level + lax.div(grp_at, 2 ** (level + 1))
        wanted = column_of(mergeskel_ref[pl.ds(node, 1), :])[:, 0:1]
        at = lax.broadcasted_iota(jnp.int32, (rank, 2 * rank), 1).astype(jnp.float32)
        picks.append(as_bf16(wanted == at))

    def multiply(slot):
        x_from = flip(x_at, slot // leaves)
        grp_from = flip(grp_at, slot % leaves)
        begin = pl.multiple_of((x_from * leaves + grp_from) * depth, 128)
        left = cols[:, :, pl.ds(begin, depth)].reshape(2 * rows, depth)
        right = omega_ref[...] if slot == 0 else slots[slot]
        acc[...] += jnp.dot(left, right, preferred_element_type=jnp.float32)

    held = {}
    ready = False
    waiting = []
    for number, (part, slot, onward) in enumerate(sequence):
        if slot != 0:
            arrivals[part, slot].wait_recv()
            for dim in onward:
                arrivals[part, slot ^ dim] = start(part, slot, dim)
        held[slot] = held.get(slot, 0) + 1
        if held[slot] == CUTS:
            waiting.append(slot)
        if number >= len(sequence) // 4:
            if not ready:
                for copy in mine:
                    copy.wait()
                for copy in given:
                    copy.wait_recv()
                ready = True
            for item in waiting:
                multiply(item)
            waiting = []

    final = pltpu.make_async_remote_copy(
        src_ref=acc.at[pl.ds(rows, rows), :],
        dst_ref=partial,
        send_sem=psem.at[0],
        recv_sem=psem.at[1],
        device_id=sibling,
        device_id_type=MESH,
    )
    final.start()
    final.wait_recv()
    sketch = (acc[pl.ds(0, rows), :] + partial[...]).astype(jnp.bfloat16)

    placed = jnp.dot(placing, sketch, preferred_element_type=jnp.float32).reshape(devices, lines, width)
    line = lax.broadcasted_iota(jnp.int32, (devices, lines, 128), 1)
    chunk_at = lax.div(line, capacity)
    sent = placed[:, :, :128]
    for chunk in range(1, chunks):
        sent = jnp.where(chunk_at == chunk, placed[:, :, chunk * 128 : (chunk + 1) * 128], sent)
    packed[...] = sent.astype(jnp.bfloat16)

    def deliver(step):
        number = lax.rem(myself + step, devices)
        return pltpu.make_async_remote_copy(
            src_ref=packed.at[number],
            dst_ref=arrived.at[myself],
            send_sem=asend.at[step],
            recv_sem=arecv.at[step],
            device_id=device(number),
            device_id_type=MESH,
        )

    def deliver_start(step, carry):
        deliver(step).start()
        return carry

    lax.fori_loop(1, devices, deliver_start, 0)
    arrived[pl.ds(myself, 1)] = packed[pl.ds(myself, 1)]

    def deliver_wait(step, carry):
        number = lax.rem(myself + devices - step, devices)
        pltpu.make_async_remote_copy(
            src_ref=packed.at[number],
            dst_ref=arrived.at[number],
            send_sem=asend.at[step],
            recv_sem=arecv.at[step],
            device_id=device(number),
            device_id_type=MESH,
        ).wait_recv()
        return carry

    lax.fori_loop(1, devices, deliver_wait, 0)
    flat = arrived[...].astype(jnp.float32)
    wide = [jnp.where(chunk_at == chunk, flat, 0.0) for chunk in range(chunks)]
    landed = jnp.concatenate(wide, axis=2).reshape(devices * lines, width).astype(jnp.bfloat16)

    eye_row = lax.broadcasted_iota(jnp.int32, (rank, rank), 0)
    ident = (eye_row == lax.broadcasted_iota(jnp.int32, (rank, rank), 1)).astype(jnp.float32)

    def offer(level, basis):
        bases[level] = basis
        side = lax.rem(lax.div(grp_at, 2**level), 2)
        place = pl.ds(pl.multiple_of(side * rank, rank), rank)
        stacks[level, place, :] = basis
        copy = pltpu.make_async_remote_copy(
            src_ref=stacks.at[level, place, :],
            dst_ref=stacks.at[level, place, :],
            send_sem=lsend.at[level],
            recv_sem=lrecv.at[level],
            device_id=(front_at, flip(grp_at, 2**level)),
            device_id_type=MESH,
        )
        copy.start()
        return copy

    def begin_solve(at):
        basis = bases[at]
        gram = lax.dot_general(
            basis, basis, (((1,), (1,)), ((), ())), precision=HIGHEST, preferred_element_type=jnp.float32
        )
        shift = 0.1 * (jnp.sum(gram * ident, keepdims=True) / rank) + 1e-05
        gram = gram + shift * ident
        scale = 1.0 / jnp.sum(gram * ident, keepdims=True)
        grams[at] = gram
        rest = ident - gram * scale
        state[at, pl.ds(0, rank), :] = (ident + rest) * scale
        state[at, pl.ds(rank, rank), :] = split_dot(rest, rest)

    def advance(systems, count):
        def step(_, carry):
            for at in systems:
                now = state[at]
                grown = split_dot(now, now[rank:])
                state[at, pl.ds(0, rank), :] = now[:rank] + grown[:rank]
                state[at, pl.ds(rank, rank), :] = grown[rank:]
            return carry

        lax.fori_loop(0, count, step, 0)

    def lift(systems):
        approx = {at: state[at, pl.ds(0, rank), :] for at in systems}
        for _ in range(EXACT_STEPS):
            inner = {at: 2.0 * ident - full_dot(grams[at], approx[at]) for at in systems}
            approx = {at: full_dot(approx[at], inner[at]) for at in systems}
        return {at: full_dot(jnp.transpose(bases[at]), approx[at]) for at in systems}

    total = STEPS - EXACT_STEPS - 1
    early = total // 2
    late = total - early
    copy = offer(0, jnp.dot(chosen, landed, preferred_element_type=jnp.float32))
    copies = [copy]
    begin_solve(0)
    advance([0], early)
    for level in range(LEVELS):
        copies[level].wait_recv()
        basis = take_rows(picks[level], stacks[level])
        if level < LEVELS - 1:
            copies.append(offer(level + 1, basis))
        else:
            bases[LEVELS] = basis
            top_ref[...] = basis
        begin_solve(level + 1)
        advance([level, level + 1], late if level != 1 else early)
        if level == 0:
            lifted = lift([0])[0]
            small = halves(jnp.dot(landed, jnp.concatenate(split(lifted), axis=1), preferred_element_type=jnp.float32))
            small = jnp.concatenate(split(small), axis=1)
            spot = lax.broadcasted_iota(jnp.int32, (leaf_ref.shape[0], devices * lines), 0).astype(jnp.float32)
            leaf_ref[...] = halves(jnp.dot(as_bf16(spot == where_to), small, preferred_element_type=jnp.float32))
        if level == 1:
            pass
    advance([LEVELS], early)
    lifted = lift(list(range(1, LEVELS + 1)))
    for level in range(LEVELS):
        node_ref[level] = split_dot(stacks[level], lifted[level + 1])

    for copy in given + list(arrivals.values()) + [final] + copies:
        copy.wait_send()

    def deliver_end(step, carry):
        deliver(step).wait_send()
        return carry

    lax.fori_loop(1, devices, deliver_end, 0)


def local(
    contributions,
    sketch_matrix,
    destinations,
    parent_rows,
    front_sizes,
    leaf_skeleton,
    merge_skeleton,
):
    fronts, leaves = lax.axis_size("front"), lax.axis_size("grp")
    devices = fronts * leaves
    rows, order = contributions.shape
    depth, width = sketch_matrix.shape
    rank = leaf_skeleton.shape[-1]
    count = devices // 2
    capacity = 2 * rows // devices
    lines = -(-capacity * (width // 128) // 16) * 16
    vmem = pl.BlockSpec(memory_space=pltpu.VMEM)
    semaphores = [
        (fronts // 2,), (fronts // 2,), (fronts // 2,), (CUTS, count), (CUTS, count), (2,),
        (devices,), (devices,), (LEVELS,), (LEVELS,),
    ]
    leaf_map, node_maps, top_rows = pl.pallas_call(
        functools.partial(whole_kernel, fronts, leaves, capacity),
        out_shape=(
            jax.ShapeDtypeStruct((PR_DEV, rank), jnp.float32),
            jax.ShapeDtypeStruct((LEVELS, 2 * rank, rank), jnp.float32),
            jax.ShapeDtypeStruct((rank, width), jnp.float32),
        ),
        in_specs=[pl.BlockSpec(memory_space=pltpu.HBM)] + [vmem] * 6,
        out_specs=(vmem, vmem, vmem),
        scratch_shapes=[
            pltpu.VMEM((2, rows, order // 2), jnp.bfloat16),
            pltpu.VMEM((count, depth, width), jnp.bfloat16),
            pltpu.VMEM((2 * rows, width), jnp.float32),
            pltpu.VMEM((rows, width), jnp.float32),
            pltpu.VMEM((devices, lines, 128), jnp.bfloat16),
            pltpu.VMEM((devices, lines, 128), jnp.bfloat16),
            pltpu.VMEM((LEVELS, 2 * rank, width), jnp.float32),
            pltpu.VMEM((LEVELS + 1, rank, width), jnp.float32),
            pltpu.VMEM((LEVELS + 1, rank, rank), jnp.float32),
            pltpu.VMEM((LEVELS + 1, 2 * rank, rank), jnp.float32),
        ]
        + [pltpu.SemaphoreType.DMA(shape) for shape in semaphores],
        compiler_params=pltpu.CompilerParams(
            collective_id=0, has_side_effects=True, vmem_limit_bytes=40 * 2**20
        ),
        cost_estimate=pl.CostEstimate(
            flops=2 * rows * order * width, bytes_accessed=2 * rows * order, transcendentals=0
        ),
    )(
        contributions,
        sketch_matrix,
        destinations.reshape(devices, rows),
        parent_rows.reshape(devices, rows),
        jnp.broadcast_to(front_sizes[None, :], (1, rows)),
        leaf_skeleton[0],
        merge_skeleton[0],
    )
    return (leaf_map[None], node_maps[None, None], top_rows[None, None])


def solution(mesh):
    in_specs = (
        P(("front", "grp"), None),
        P(("front", "grp"), None),
        P(),
        P(),
        P("front"),
        P("front", "grp", None),
        P("front", None, None),
    )
    out_specs = (
        P("front", "grp", None),
        P("front", "grp", None, None, None),
        P("front", "grp", None, None),
    )
    return jax.shard_map(local, mesh=mesh, in_specs=in_specs, out_specs=out_specs, check_vma=False)
```

time: 184 us -> 84.6 us (0.46)
  waiting for transfers between devices: 84.4 us -> 0 us
  Pallas kernels: 0 us -> 74.8 us
  matrix products: 53.1 us -> 0 us
  between operations: 21.9 us -> 1.3 us
  other arithmetic: 10.5 us -> 0 us
  starting transfers between devices: 6.78 us -> 0 us
    all_gather x1 -> x0, waiting for transfers between devices: 77.6 us -> none  [local(): lax.all_gather(sketch_matrix, ('front', 'grp'), axis=0, tiled=True)]
    pallas_call x0 -> x1, Pallas kernels: none -> 74.8 us  [local(): pl.pallas_call(functools.partial(whole_kernel, fronts, leaves, capacity),...]
    dot_general x210 -> x0, matrix products: 53.1 us -> none  [the longest x96 19.7 us: ridge_map(): jnp.dot(gram, approx, precision=lax.Precision.HIGHEST)]
    unnamed x4 -> x14, local copies, waits for them, and re-layouts: 0.01 us -> 8.11 us
    reduce_sum x10 -> x0, other arithmetic: 6.92 us -> none  [the longest x4 2.48 us: ridge_map(): approx = ident / jnp.trace(gram)]
    all_to_all x1 -> x0, waiting for transfers between devices: 6.08 us -> none  [local(): lax.all_to_all(packed, ('front', 'grp'), split_axis=0, concat_axis=0, til...]
    gather x4 -> x0, local copies, waits for them, and re-layouts: 5.76 us -> none  [ridge_map(): shift = 0.1 * jnp.mean(jnp.diagonal(gram)) + 1e-05]
    ppermute x3 -> x0, starting transfers between devices: 3.37 us -> none  [from_partner(): return lax.ppermute(block, axis, route)]
  transfers between devices with their start and end apart: 5 -> 0, of which waited for: 2 -> 0; matrix products, arithmetic and copies ran while one was open for 25% -> 0% of each run, Pallas kernels for 0% -> 0%
where the time goes in v2:
time: 84.6 us; the launch traced here: 84.2 us
  Pallas kernels  74.8 us (88%)
  local copies, waits for them, and re-layouts  8.11 us (10%)
  between operations  1.3 us (2%)
    pallas_call x1, Pallas kernels, local(): pl.pallas_call(functools.partial(whole_kernel, fronts, leaves, capacity),...  74.8 us
    unnamed x14, local copies, waits for them, and re-layouts  8.11 us

profile of v2, /device:TPU:0, one launch (start us, length us, event | category | flops | bytes accessed | tf_op | source)
XLA Modules:
  0.0 84.2 jit_solution(4761436364302616025)
XLA Ops:
  1.3 0.7 copy.12
  2.0 0.0 copy-start
  2.0 2.2 %copy-done = bf16[128,16384]{1,0:T(8,128)(2,1)S(1)} copy-done((bf16[128,16384]{1,0:T(8,128)(2,1)S(1)}, bf16[128,16384]{1,0:T(8,128)(2,1)}, u32[]{:S(2)}) %copy-start) | copy-done | bytes 4194328
  4.2 0.0 copy-start.1
  4.2 0.9 %copy-done.1 = bf16[512,256]{1,0:T(8,128)(2,1)S(1)} copy-done((bf16[512,256]{1,0:T(8,128)(2,1)S(1)}, bf16[512,256]{1,0:T(8,128)(2,1)}, u32[]{:S(2)}) %copy-start.1) | copy-done | bytes 262168
  5.1 0.0 copy-start.2
  5.1 0.7 copy-done.2
  5.8 0.0 copy-start.3
  5.8 0.7 copy-done.3
  6.6 0.0 copy-start.4
  6.6 0.7 copy-done.4
  7.2 74.8 %shard_map.94 = (f32[1024,128]{1,0:T(8,128)S(1)}, f32[3,256,128]{2,1,0:T(8,128)S(1)}, f32[128,256]{1,0:T(8,128)S(1)}) custom-call(bf16[128,16384]{1,0:T(8,128)(2,1)S(1)} %copy-done, bf16[512,256]{1,0:T(8,128)(2,1)S(1)} %copy-done.1, s32[32,128]{1,0:T(8,128)S(1)} %bitcast.14, s32[32,128]{1,0:T(8,128)S(1)} %bitcast.15, ...), custom_call_target="tpu_custom_call" | custom-call | flops 1073741824 | bytes 4194304 | tf_op jit(solution)/shard_map/pallas_call | solution.py:410
  82.0 0.8 copy.17
  82.8 0.7 copy.18
  83.6 0.7 copy.19
  (1 shorter events, 0.0 us)
Async XLA Ops:
  2.0 2.2 %copy-start = (bf16[128,16384]{1,0:T(8,128)(2,1)S(1)}, bf16[128,16384]{1,0:T(8,128)(2,1)}, u32[]{:S(2)}) copy-start(bf16[128,16384]{1,0:T(8,128)(2,1)} %c_ref.1) | copy-start | bytes 12582916
  4.2 0.9 %copy-start.1 = (bf16[512,256]{1,0:T(8,128)(2,1)S(1)}, bf16[512,256]{1,0:T(8,128)(2,1)}, u32[]{:S(2)}) copy-start(bf16[512,256]{1,0:T(8,128)(2,1)} %omega_ref.1) | copy-start | bytes 786436
  5.1 0.7 copy-start.2
  5.8 0.7 copy-start.3
  6.6 0.7 copy-start.4

commit v3 on v2

--- a/solution.py
+++ b/solution.py
@@ -11,7 +11,7 @@
 PR_DEV = 1024
 LEVELS = 3
 STEPS = 24
-EXACT_STEPS = 2
+EXACT_STEPS = 1
 CUTS = 4
 HIGHEST = lax.Precision.HIGHEST
 MESH = pl.DeviceIdType.MESH
@@ -97,10 +97,11 @@
 
 def whole_kernel(
     fronts, leaves, capacity,
-    c_ref, omega_ref, dest_ref, prow_ref, size_ref, leafskel_ref, mergeskel_ref,
-    leaf_ref, node_ref, top_ref,
+    c_ref, omega_ref, dest_hbm, prow_hbm, size_hbm, leafskel_hbm, mergeskel_hbm,
+    leaf_hbm, node_hbm, top_hbm,
+    dest_ref, prow_ref, size_ref, leafskel_ref, mergeskel_ref, leaf_ref, node_ref,
     cols, slots, acc, partial, packed, arrived, stacks, bases, grams, state,
-    local_sem, csend, crecv, send, recv, psem, asend, arecv, lsend, lrecv,
+    local_sem, table_sem, out_sem, csend, crecv, send, recv, psem, asend, arecv, lsend, lrecv,
 ):
     front_at = lax.axis_index("front")
     grp_at = lax.axis_index("grp")
@@ -125,6 +126,11 @@
             return (front_at, flip(grp_at, dim))
         return (flip(x_at, dim // leaves) * 2 + core, grp_at)
 
+    tables = [
+        (dest_hbm, dest_ref), (prow_hbm, prow_ref), (size_hbm, size_ref),
+        (leafskel_hbm, leafskel_ref), (mergeskel_hbm, mergeskel_ref),
+    ]
+    tables = [pltpu.make_async_copy(a, b, table_sem.at[at]) for at, (a, b) in enumerate(tables)]
     barrier = pltpu.get_barrier_semaphore()
 
     def greet(step, carry):
@@ -141,6 +147,11 @@
         )
         copy.start()
         mine.append(copy)
+    copy = pltpu.make_async_copy(omega_ref, slots.at[0], local_sem.at[x_count])
+    copy.start()
+    mine.append(copy)
+    for copy in tables:
+        copy.start()
     pl.semaphore_wait(barrier, devices - 1)
 
     def start(part, slot, dim):
@@ -181,44 +192,50 @@
     chunks = width // 128
     used = capacity * chunks
     lines = packed.shape[1]
-    shape = (devices, lines, rows)
-    block_at = lax.broadcasted_iota(jnp.int32, shape, 0).astype(jnp.float32)
-    line_at = lax.broadcasted_iota(jnp.int32, shape, 1)
-    slot_at = jnp.where(line_at < used, lax.rem(line_at, capacity), -1).astype(jnp.float32)
-    row = lax.broadcasted_iota(jnp.int32, (rows, rows), 0)
-    col = lax.broadcasted_iota(jnp.int32, (rows, rows), 1)
-    going = dest_ref[pl.ds(myself, 1), :].astype(jnp.float32)
-    same = (column_of(going)[:, :rows] == going) & (row < col)
-    rank_in = jnp.sum(same.astype(jnp.float32), axis=0, keepdims=True)
-    placing = as_bf16((block_at == going.reshape(1, 1, rows)) & (slot_at == rank_in.reshape(1, 1, rows)))
-    placing = placing.reshape(devices * lines, rows)
-
-    coming = dest_ref[...] == myself
-    ahead = jnp.dot(as_bf16(coming), as_bf16(row < col), preferred_element_type=jnp.float32)
-    ahead = jnp.where(coming, ahead, -2.0)
-    live = prow_ref[...] + grp_at * PR_DEV < size_ref[...]
-    landing = jnp.where(live, prow_ref[...] + 1, 0).astype(jnp.float32)
-    hit = ahead.reshape(devices, 1, rows) == slot_at
-    where_to = jnp.sum(jnp.where(hit, landing.reshape(devices, 1, rows), 0.0), axis=2, keepdims=True) - 1.0
-    where_to = where_to.reshape(devices * lines, 1)
-    where_to = jnp.transpose(jnp.broadcast_to(where_to, (devices * lines, 128)))[0:1, :]
-    chosen = as_bf16(column_of(leafskel_ref[...])[:, 0:1] == where_to)
-    picks = []
-    for level in range(LEVELS):
-        node = leaves - leaves // 2**level + lax.div(grp_at, 2 ** (level + 1))
-        wanted = column_of(mergeskel_ref[pl.ds(node, 1), :])[:, 0:1]
-        at = lax.broadcasted_iota(jnp.int32, (rank, 2 * rank), 1).astype(jnp.float32)
-        picks.append(as_bf16(wanted == at))
+    kept = capacity if capacity % 8 == 0 else lines
+
+    def make_tables():
+        for copy in tables:
+            copy.wait()
+        shape = (devices, lines, rows)
+        block_at = lax.broadcasted_iota(jnp.int32, shape, 0).astype(jnp.float32)
+        line_at = lax.broadcasted_iota(jnp.int32, shape, 1)
+        slot_at = jnp.where(line_at < used, lax.rem(line_at, capacity), -1).astype(jnp.float32)
+        row = lax.broadcasted_iota(jnp.int32, (rows, rows), 0)
+        col = lax.broadcasted_iota(jnp.int32, (rows, rows), 1)
+        going = dest_ref[pl.ds(myself, 1), :].astype(jnp.float32)
+        same = (column_of(going)[:, :rows] == going) & (row < col)
+        rank_in = jnp.sum(same.astype(jnp.float32), axis=0, keepdims=True)
+        placing = as_bf16((block_at == going.reshape(1, 1, rows)) & (slot_at == rank_in.reshape(1, 1, rows)))
+        placing = placing.reshape(devices * lines, rows)
+
+        coming = dest_ref[...] == myself
+        ahead = jnp.dot(as_bf16(coming), as_bf16(row < col), preferred_element_type=jnp.float32)
+        ahead = jnp.where(coming, ahead, -2.0)
+        live = prow_ref[...] + grp_at * PR_DEV < size_ref[...]
+        landing = jnp.where(live, prow_ref[...] + 1, 0).astype(jnp.float32)
+        hit = ahead.reshape(devices, 1, rows) == slot_at[:, :kept, :]
+        where_to = jnp.sum(jnp.where(hit, landing.reshape(devices, 1, rows), 0.0), axis=2, keepdims=True) - 1.0
+        where_to = where_to.reshape(devices * kept, 1)
+        where_to = jnp.transpose(jnp.broadcast_to(where_to, (devices * kept, 128)))[0:1, :]
+        chosen = as_bf16(column_of(leafskel_ref[...])[:, 0:1] == where_to)
+        picks = []
+        for level in range(LEVELS):
+            node = leaves - leaves // 2**level + lax.div(grp_at, 2 ** (level + 1))
+            wanted = column_of(mergeskel_ref[node])[:, 0:1]
+            at = lax.broadcasted_iota(jnp.int32, (rank, 2 * rank), 1).astype(jnp.float32)
+            picks.append(as_bf16(wanted == at))
+        return placing, where_to, chosen, picks
 
     def multiply(slot):
         x_from = flip(x_at, slot // leaves)
         grp_from = flip(grp_at, slot % leaves)
         begin = pl.multiple_of((x_from * leaves + grp_from) * depth, 128)
         left = cols[:, :, pl.ds(begin, depth)].reshape(2 * rows, depth)
-        right = omega_ref[...] if slot == 0 else slots[slot]
-        acc[...] += jnp.dot(left, right, preferred_element_type=jnp.float32)
+        acc[...] += jnp.dot(left, slots[slot], preferred_element_type=jnp.float32)
 
     held = {}
+    forwards = max(at for at, item in enumerate(sequence) if item[2])
     ready = False
     waiting = []
     for number, (part, slot, onward) in enumerate(sequence):
@@ -236,9 +253,12 @@
                 for copy in given:
                     copy.wait_recv()
                 ready = True
-            for item in waiting:
-                multiply(item)
-            waiting = []
+            if waiting:
+                multiply(waiting.pop(0))
+        if number == forwards:
+            placing, where_to, chosen, picks = make_tables()
+    for item in waiting:
+        multiply(item)
 
     final = pltpu.make_async_remote_copy(
         src_ref=acc.at[pl.ds(rows, rows), :],
@@ -292,8 +312,11 @@
 
     lax.fori_loop(1, devices, deliver_wait, 0)
     flat = arrived[...].astype(jnp.float32)
-    wide = [jnp.where(chunk_at == chunk, flat, 0.0) for chunk in range(chunks)]
-    landed = jnp.concatenate(wide, axis=2).reshape(devices * lines, width).astype(jnp.bfloat16)
+    if kept == capacity:
+        wide = [flat[:, chunk * capacity : (chunk + 1) * capacity] for chunk in range(chunks)]
+    else:
+        wide = [jnp.where(chunk_at == chunk, flat, 0.0) for chunk in range(chunks)]
+    landed = jnp.concatenate(wide, axis=2).reshape(devices * kept, width).astype(jnp.bfloat16)
 
     eye_row = lax.broadcasted_iota(jnp.int32, (rank, rank), 0)
     ident = (eye_row == lax.broadcasted_iota(jnp.int32, (rank, rank), 1)).astype(jnp.float32)
@@ -338,20 +361,52 @@
 
         lax.fori_loop(0, count, step, 0)
 
-    def lift(systems):
+    def refine(systems):
         approx = {at: state[at, pl.ds(0, rank), :] for at in systems}
         for _ in range(EXACT_STEPS):
             inner = {at: 2.0 * ident - full_dot(grams[at], approx[at]) for at in systems}
             approx = {at: full_dot(approx[at], inner[at]) for at in systems}
+        return approx
+
+    def lift(systems, approx):
         return {at: full_dot(jnp.transpose(bases[at]), approx[at]) for at in systems}
 
+    def put(source, target, at):
+        copy = pltpu.make_async_copy(source, target, out_sem.at[at])
+        copy.start()
+        return copy
+
+    def write_leaf(lifted):
+        small = halves(jnp.dot(landed, jnp.concatenate(split(lifted), axis=1), preferred_element_type=jnp.float32))
+        small = jnp.concatenate(split(small), axis=1)
+        spot = lax.broadcasted_iota(jnp.int32, (leaf_ref.shape[0], devices * kept), 0).astype(jnp.float32)
+        leaf_ref[...] = halves(jnp.dot(as_bf16(spot == where_to), small, preferred_element_type=jnp.float32))
+        outputs.append(put(leaf_ref, leaf_hbm, LEVELS))
+
+    def write_nodes(levels, lifted):
+        for level in levels:
+            node_ref[level] = split_dot(stacks[level], lifted[level + 1])
+        for level in levels:
+            outputs.append(put(node_ref.at[level], node_hbm.at[level], level))
+
+    def end_sends():
+        for copy in given + list(arrivals.values()) + [final]:
+            copy.wait_send()
+
+        def deliver_end(step, carry):
+            deliver(step).wait_send()
+            return carry
+
+        lax.fori_loop(1, devices, deliver_end, 0)
+
+    outputs = []
     total = STEPS - EXACT_STEPS - 1
     early = total // 2
     late = total - early
-    copy = offer(0, jnp.dot(chosen, landed, preferred_element_type=jnp.float32))
-    copies = [copy]
+    copies = [offer(0, jnp.dot(chosen, landed, preferred_element_type=jnp.float32))]
     begin_solve(0)
     advance([0], early)
+    end_sends()
     for level in range(LEVELS):
         copies[level].wait_recv()
         basis = take_rows(picks[level], stacks[level])
@@ -359,30 +414,32 @@
             copies.append(offer(level + 1, basis))
         else:
             bases[LEVELS] = basis
-            top_ref[...] = basis
+            outputs.append(put(bases.at[LEVELS], top_hbm, LEVELS + 1))
         begin_solve(level + 1)
-        advance([level, level + 1], late if level != 1 else early)
         if level == 0:
-            lifted = lift([0])[0]
-            small = halves(jnp.dot(landed, jnp.concatenate(split(lifted), axis=1), preferred_element_type=jnp.float32))
-            small = jnp.concatenate(split(small), axis=1)
-            spot = lax.broadcasted_iota(jnp.int32, (leaf_ref.shape[0], devices * lines), 0).astype(jnp.float32)
-            leaf_ref[...] = halves(jnp.dot(as_bf16(spot == where_to), small, preferred_element_type=jnp.float32))
-        if level == 1:
-            pass
-    advance([LEVELS], early)
-    lifted = lift(list(range(1, LEVELS + 1)))
-    for level in range(LEVELS):
-        node_ref[level] = split_dot(stacks[level], lifted[level + 1])
-
-    for copy in given + list(arrivals.values()) + [final] + copies:
+            advance([0, 1], late)
+        elif level == 1:
+            advance([1, 2], early)
+            write_leaf(lift([0], refine([0]))[0])
+        else:
+            advance([2, 3], late)
+    now = state[LEVELS]
+    lower = list(range(1, LEVELS))
+    for number in range(early):
+        if number == 1:
+            approx = refine(lower)
+        if number == 4:
+            lifted = lift(lower, approx)
+        if number == 6:
+            write_nodes(range(LEVELS - 1), lifted)
+        grown = split_dot(now, now[rank:])
+        now = jnp.concatenate([now[:rank] + grown[:rank], grown[rank:]], axis=0)
+    state[LEVELS] = now
+    write_nodes([LEVELS - 1], lift([LEVELS], refine([LEVELS])))
+    for copy in copies:
         copy.wait_send()
-
-    def deliver_end(step, carry):
-        deliver(step).wait_send()
-        return carry
-
-    lax.fori_loop(1, devices, deliver_end, 0)
+    for copy in outputs:
+        copy.wait()
 
 
 def local(
@@ -402,9 +459,9 @@
     count = devices // 2
     capacity = 2 * rows // devices
     lines = -(-capacity * (width // 128) // 16) * 16
-    vmem = pl.BlockSpec(memory_space=pltpu.VMEM)
+    hbm = pl.BlockSpec(memory_space=pl.ANY)
     semaphores = [
-        (fronts // 2,), (fronts // 2,), (fronts // 2,), (CUTS, count), (CUTS, count), (2,),
+        (fronts // 2 + 1,), (5,), (LEVELS + 2,), (fronts // 2,), (fronts // 2,), (CUTS, count), (CUTS, count), (2,),
         (devices,), (devices,), (LEVELS,), (LEVELS,),
     ]
     leaf_map, node_maps, top_rows = pl.pallas_call(
@@ -414,9 +471,16 @@
             jax.ShapeDtypeStruct((LEVELS, 2 * rank, rank), jnp.float32),
             jax.ShapeDtypeStruct((rank, width), jnp.float32),
         ),
-        in_specs=[pl.BlockSpec(memory_space=pltpu.HBM)] + [vmem] * 6,
-        out_specs=(vmem, vmem, vmem),
+        in_specs=[hbm] * 7,
+        out_specs=(hbm, hbm, hbm),
         scratch_shapes=[
+            pltpu.VMEM((devices, rows), jnp.int32),
+            pltpu.VMEM((devices, rows), jnp.int32),
+            pltpu.VMEM((1, rows), jnp.int32),
+            pltpu.VMEM((1, rank), jnp.int32),
+            pltpu.VMEM((merge_skeleton.shape[1], 1, rank), jnp.int32),
+            pltpu.VMEM((PR_DEV, rank), jnp.float32),
+            pltpu.VMEM((LEVELS, 2 * rank, rank), jnp.float32),
             pltpu.VMEM((2, rows, order // 2), jnp.bfloat16),
             pltpu.VMEM((count, depth, width), jnp.bfloat16),
             pltpu.VMEM((2 * rows, width), jnp.float32),
@@ -430,7 +494,7 @@
         ]
         + [pltpu.SemaphoreType.DMA(shape) for shape in semaphores],
         compiler_params=pltpu.CompilerParams(
-            collective_id=0, has_side_effects=True, vmem_limit_bytes=40 * 2**20
+            collective_id=0, has_side_effects=True, vmem_limit_bytes=62 * 2**20
         ),
         cost_estimate=pl.CostEstimate(
             flops=2 * rows * order * width, bytes_accessed=2 * rows * order, transcendentals=0
@@ -442,7 +506,7 @@
         parent_rows.reshape(devices, rows),
         jnp.broadcast_to(front_sizes[None, :], (1, rows)),
         leaf_skeleton[0],
-        merge_skeleton[0],
+        merge_skeleton.reshape(merge_skeleton.shape[1], 1, rank),
     )
     return (leaf_map[None], node_maps[None, None], top_rows[None, None])
 

time: 84.6 us -> 80.7 us (0.954)
  local copies, waits for them, and re-layouts: 8.11 us -> 5.71 us
  Pallas kernels: 74.8 us -> 73.4 us
    unnamed x14 -> x3, local copies, waits for them, and re-layouts: 8.11 us -> 5.2 us
    pallas_call x1, Pallas kernels: 74.8 us -> 73.4 us  [local(): pl.pallas_call(functools.partial(whole_kernel, fronts, leaves, capacity),...]
where the time goes in v3:
time: 80.7 us; the launch traced here: 80.4 us
  Pallas kernels  73.4 us (91%)
  local copies, waits for them, and re-layouts  5.71 us (7%)
  between operations  1.29 us (2%)
    pallas_call x1, Pallas kernels, local(): pl.pallas_call(functools.partial(whole_kernel, fronts, leaves, capacity),...  73.4 us
    unnamed x3, local copies, waits for them, and re-layouts  5.2 us

profile of v3, /device:TPU:0, one launch (start us, length us, event | category | flops | bytes accessed | tf_op | source)
XLA Modules:
  0.0 80.4 jit_solution(551028940344443737)
XLA Ops:
  1.3 0.5 broadcast_in_dim.18.size_hbm
  1.8 73.4 %shard_map.94 = (f32[1024,128]{1,0:T(8,128)}, f32[3,256,128]{2,1,0:T(8,128)}, f32[128,256]{1,0:T(8,128)}) custom-call(bf16[128,16384]{1,0:T(8,128)(2,1)} %c_ref.1, bf16[512,256]{1,0:T(8,128)(2,1)} %omega_ref.1, s32[32,128]{1,0:T(8,128)} %bitcast.12, s32[32,128]{1,0:T(8,128)} %bitcast.13, s32[1,128]{1,0:T(1,128)} %broadcast_in_dim.18.size_hbm, ...), custom_call_target="tpu_custom_call" | custom-call | flops 1073741824 | bytes 4194304 | tf_op jit(solution)/shard_map/pallas_call | solution.py:467
  75.2 1.9 %copy.14 = f32[1,1024,128]{2,1,0:T(8,128)} copy(f32[1,1024,128]{2,1,0:T(8,128)} %bitcast.9) | data formatting | bytes 1048576
  77.1 1.8 %copy.15 = f32[1,1,3,256,128]{4,3,2,1,0:T(8,128)} copy(f32[1,1,3,256,128]{4,3,2,1,0:T(8,128)} %bitcast.10) | data formatting | bytes 786432
  78.9 1.6 %copy.16 = f32[1,1,128,256]{3,2,1,0:T(8,128)} copy(f32[1,1,128,256]{3,2,1,0:T(8,128)} %bitcast.11) | data formatting | bytes 262144

commit v4 on v3

--- a/solution.py
+++ b/solution.py
@@ -13,6 +13,7 @@
 STEPS = 24
 EXACT_STEPS = 1
 CUTS = 4
+SHARES = 4
 HIGHEST = lax.Precision.HIGHEST
 MESH = pl.DeviceIdType.MESH
 
@@ -212,7 +213,7 @@
         coming = dest_ref[...] == myself
         ahead = jnp.dot(as_bf16(coming), as_bf16(row < col), preferred_element_type=jnp.float32)
         ahead = jnp.where(coming, ahead, -2.0)
-        live = prow_ref[...] + grp_at * PR_DEV < size_ref[...]
+        live = prow_ref[...] + grp_at * PR_DEV < size_ref[0]
         landing = jnp.where(live, prow_ref[...] + 1, 0).astype(jnp.float32)
         hit = ahead.reshape(devices, 1, rows) == slot_at[:, :kept, :]
         where_to = jnp.sum(jnp.where(hit, landing.reshape(devices, 1, rows), 0.0), axis=2, keepdims=True) - 1.0
@@ -403,6 +404,7 @@
     total = STEPS - EXACT_STEPS - 1
     early = total // 2
     late = total - early
+    ahead = 5
     copies = [offer(0, jnp.dot(chosen, landed, preferred_element_type=jnp.float32))]
     begin_solve(0)
     advance([0], early)
@@ -420,12 +422,13 @@
             advance([0, 1], late)
         elif level == 1:
             advance([1, 2], early)
+            advance([2], ahead)
             write_leaf(lift([0], refine([0]))[0])
         else:
-            advance([2, 3], late)
+            advance([2, 3], late - ahead)
     now = state[LEVELS]
     lower = list(range(1, LEVELS))
-    for number in range(early):
+    for number in range(early + ahead):
         if number == 1:
             approx = refine(lower)
         if number == 4:
@@ -439,6 +442,20 @@
     for copy in copies:
         copy.wait_send()
     for copy in outputs:
+        copy.wait()
+
+
+def hand_on(*refs):
+    sources, targets, sem = refs[:3], refs[3:6], refs[6]
+    copies = []
+    for at, (source, target) in enumerate(zip(sources, targets)):
+        share = source.shape[-2] // SHARES
+        for part in range(SHARES):
+            place = (slice(None),) * (len(source.shape) - 2) + (pl.ds(part * share, share),)
+            copies.append(pltpu.make_async_copy(source.at[place], target.at[place], sem.at[at, part]))
+    for copy in copies:
+        copy.start()
+    for copy in copies:
         copy.wait()
 
 
@@ -464,7 +481,7 @@
         (fronts // 2 + 1,), (5,), (LEVELS + 2,), (fronts // 2,), (fronts // 2,), (CUTS, count), (CUTS, count), (2,),
         (devices,), (devices,), (LEVELS,), (LEVELS,),
     ]
-    leaf_map, node_maps, top_rows = pl.pallas_call(
+    results = pl.pallas_call(
         functools.partial(whole_kernel, fronts, leaves, capacity),
         out_shape=(
             jax.ShapeDtypeStruct((PR_DEV, rank), jnp.float32),
@@ -476,7 +493,7 @@
         scratch_shapes=[
             pltpu.VMEM((devices, rows), jnp.int32),
             pltpu.VMEM((devices, rows), jnp.int32),
-            pltpu.VMEM((1, rows), jnp.int32),
+            pltpu.SMEM((1,), jnp.int32),
             pltpu.VMEM((1, rank), jnp.int32),
             pltpu.VMEM((merge_skeleton.shape[1], 1, rank), jnp.int32),
             pltpu.VMEM((PR_DEV, rank), jnp.float32),
@@ -504,10 +521,18 @@
         sketch_matrix,
         destinations.reshape(devices, rows),
         parent_rows.reshape(devices, rows),
-        jnp.broadcast_to(front_sizes[None, :], (1, rows)),
+        front_sizes,
         leaf_skeleton[0],
         merge_skeleton.reshape(merge_skeleton.shape[1], 1, rank),
     )
+    leaf_map, node_maps, top_rows = pl.pallas_call(
+        hand_on,
+        out_shape=[jax.ShapeDtypeStruct(result.shape, result.dtype) for result in results],
+        in_specs=[hbm] * 3,
+        out_specs=[hbm] * 3,
+        scratch_shapes=[pltpu.SemaphoreType.DMA((3, SHARES))],
+        compiler_params=pltpu.CompilerParams(vmem_limit_bytes=62 * 2**20),
+    )(*results)
     return (leaf_map[None], node_maps[None, None], top_rows[None, None])
 
 

time: 80.7 us -> 109 us (1.35)
  Pallas kernels: 73.4 us -> 107 us
  local copies, waits for them, and re-layouts: 5.71 us -> 0 us
    pallas_call x0 -> x1, Pallas kernels: none -> 33 us  [local(): pl.pallas_call(hand_on, out_shape=[jax.ShapeDtypeStruct(result.shape, res...]
    unnamed x3 -> x0, local copies, waits for them, and re-layouts: 5.2 us -> none
where the time goes in v4:
time: 109 us; the launch traced here: 108 us
  Pallas kernels  107 us (98%)
  between operations  1.29 us (1%)
    pallas_call x1, Pallas kernels, local(): pl.pallas_call(functools.partial(whole_kernel, fronts, leaves, capacity),...  74.1 us
    pallas_call x1, Pallas kernels, local(): pl.pallas_call(hand_on, out_shape=[jax.ShapeDtypeStruct(result.shape, res...  33 us

profile of v4, /device:TPU:0, one launch (start us, length us, event | category | flops | bytes accessed | tf_op | source)
XLA Modules:
  0.0 108.4 jit_solution(8957548387875537903)
XLA Ops:
  1.3 74.1 %shard_map.94 = (f32[1024,128]{1,0:T(8,128)}, f32[3,256,128]{2,1,0:T(8,128)}, f32[128,256]{1,0:T(8,128)}) custom-call(bf16[128,16384]{1,0:T(8,128)(2,1)} %c_ref.1, bf16[512,256]{1,0:T(8,128)(2,1)} %omega_ref.1, s32[32,128]{1,0:T(8,128)} %bitcast.7, s32[32,128]{1,0:T(8,128)} %bitcast.8, s32[1]{0:T(128)S(6)} %copy.10.size_hbm, s32[1,128]{1,0:T(1,128)} %bitcast.10, ...), custom_call_target="tpu_custom_call" | custom-call | flops 1073741824 | bytes 4194304 | tf_op jit(solution)/shard_map/pallas_call | solution.py:484
  75.4 33.0 %shard_map.95 = (f32[1024,128]{1,0:T(8,128)}, f32[3,256,128]{2,1,0:T(8,128)}, f32[128,256]{1,0:T(8,128)}) custom-call(f32[1024,128]{1,0:T(8,128)} %get-tuple-element.9.refs_0_, f32[3,256,128]{2,1,0:T(8,128)} %get-tuple-element.10.refs_1_, f32[128,256]{1,0:T(8,128)} %get-tuple-element.11.refs_2_), custom_call_target="tpu_custom_call" | custom-call | tf_op jit(solution)/shard_map/pallas_call | solution.py:528

commit v5 on v4

--- a/solution.py
+++ b/solution.py
@@ -299,6 +299,10 @@
     lax.fori_loop(1, devices, deliver_start, 0)
     arrived[pl.ds(myself, 1)] = packed[pl.ds(myself, 1)]
 
+    def deliver_end(step, carry):
+        deliver(step).wait_send()
+        return carry
+
     def deliver_wait(step, carry):
         number = lax.rem(myself + devices - step, devices)
         pltpu.make_async_remote_copy(
@@ -311,6 +315,8 @@
         ).wait_recv()
         return carry
 
+    for copy in given + list(arrivals.values()) + [final]:
+        copy.wait_send()
     lax.fori_loop(1, devices, deliver_wait, 0)
     flat = arrived[...].astype(jnp.float32)
     if kept == capacity:
@@ -322,21 +328,31 @@
     eye_row = lax.broadcasted_iota(jnp.int32, (rank, rank), 0)
     ident = (eye_row == lax.broadcasted_iota(jnp.int32, (rank, rank), 1)).astype(jnp.float32)
 
-    def offer(level, basis):
-        bases[level] = basis
+    def offer(level, chunk, basis):
         side = lax.rem(lax.div(grp_at, 2**level), 2)
         place = pl.ds(pl.multiple_of(side * rank, rank), rank)
-        stacks[level, place, :] = basis
+        columns = pl.ds(chunk * 128, 128)
+        bases[level, :, columns] = basis
+        stacks[level, place, columns] = basis
         copy = pltpu.make_async_remote_copy(
-            src_ref=stacks.at[level, place, :],
-            dst_ref=stacks.at[level, place, :],
-            send_sem=lsend.at[level],
-            recv_sem=lrecv.at[level],
+            src_ref=stacks.at[level, place, columns],
+            dst_ref=stacks.at[level, place, columns],
+            send_sem=lsend.at[level, chunk],
+            recv_sem=lrecv.at[level, chunk],
             device_id=(front_at, flip(grp_at, 2**level)),
             device_id_type=MESH,
         )
         copy.start()
-        return copy
+        copies[level, chunk] = copy
+
+    def merge(level, chunk):
+        copies[level, chunk].wait_recv()
+        columns = pl.ds(chunk * 128, 128)
+        basis = take_rows(picks[level], stacks[level, :, columns])
+        if level < LEVELS - 1:
+            offer(level + 1, chunk, basis)
+        else:
+            bases[LEVELS, :, columns] = basis
 
     def begin_solve(at):
         basis = bases[at]
@@ -390,72 +406,72 @@
         for level in levels:
             outputs.append(put(node_ref.at[level], node_hbm.at[level], level))
 
-    def end_sends():
-        for copy in given + list(arrivals.values()) + [final]:
-            copy.wait_send()
-
-        def deliver_end(step, carry):
-            deliver(step).wait_send()
-            return carry
-
-        lax.fori_loop(1, devices, deliver_end, 0)
-
     outputs = []
+    copies = {}
     total = STEPS - EXACT_STEPS - 1
-    early = total // 2
-    late = total - early
-    ahead = 5
-    copies = [offer(0, jnp.dot(chosen, landed, preferred_element_type=jnp.float32))]
+    first, second, third = total // 4, total // 7, total // 10
+    leaf_basis = jnp.dot(chosen, landed, preferred_element_type=jnp.float32)
+    for chunk in range(chunks):
+        offer(0, chunk, leaf_basis[:, chunk * 128 : (chunk + 1) * 128])
     begin_solve(0)
-    advance([0], early)
-    end_sends()
-    for level in range(LEVELS):
-        copies[level].wait_recv()
-        basis = take_rows(picks[level], stacks[level])
-        if level < LEVELS - 1:
-            copies.append(offer(level + 1, basis))
-        else:
-            bases[LEVELS] = basis
-            outputs.append(put(bases.at[LEVELS], top_hbm, LEVELS + 1))
-        begin_solve(level + 1)
-        if level == 0:
-            advance([0, 1], late)
-        elif level == 1:
-            advance([1, 2], early)
-            advance([2], ahead)
-            write_leaf(lift([0], refine([0]))[0])
-        else:
-            advance([2, 3], late - ahead)
+    advance([0], first)
+    for chunk in range(chunks):
+        merge(0, chunk)
+        if chunk == 0:
+            advance([0], second)
+    begin_solve(1)
+    for chunk in range(chunks):
+        merge(1, chunk)
+        if chunk == 0:
+            advance([0, 1], third)
+    begin_solve(2)
+    left = total - first - second - third
+    advance([0, 1, 2], left)
+    lax.fori_loop(1, devices, deliver_end, 0)
+    for chunk in range(chunks):
+        merge(2, chunk)
+    outputs.append(put(bases.at[LEVELS], top_hbm, LEVELS + 1))
+    begin_solve(3)
+    more = total - third - left
+    advance([1, 2, 3], more)
+    rest = total - left - more
+    advance([2, 3], rest)
     now = state[LEVELS]
-    lower = list(range(1, LEVELS))
-    for number in range(early + ahead):
+    lower = list(range(LEVELS))
+    for number in range(total - more - rest):
         if number == 1:
             approx = refine(lower)
         if number == 4:
             lifted = lift(lower, approx)
         if number == 6:
+            write_leaf(lifted[0])
+        if number == 8:
             write_nodes(range(LEVELS - 1), lifted)
         grown = split_dot(now, now[rank:])
         now = jnp.concatenate([now[:rank] + grown[:rank], grown[rank:]], axis=0)
     state[LEVELS] = now
     write_nodes([LEVELS - 1], lift([LEVELS], refine([LEVELS])))
-    for copy in copies:
+    for copy in copies.values():
         copy.wait_send()
     for copy in outputs:
         copy.wait()
 
 
 def hand_on(*refs):
-    sources, targets, sem = refs[:3], refs[3:6], refs[6]
-    copies = []
-    for at, (source, target) in enumerate(zip(sources, targets)):
+    sources, targets, held, sem = refs[:3], refs[3:6], refs[6:9], refs[9]
+    into, out = [], []
+    for at, (source, middle, target) in enumerate(zip(sources, held, targets)):
         share = source.shape[-2] // SHARES
         for part in range(SHARES):
             place = (slice(None),) * (len(source.shape) - 2) + (pl.ds(part * share, share),)
-            copies.append(pltpu.make_async_copy(source.at[place], target.at[place], sem.at[at, part]))
-    for copy in copies:
-        copy.start()
-    for copy in copies:
+            into.append(pltpu.make_async_copy(source.at[place], middle.at[place], sem.at[0, at, part]))
+            out.append(pltpu.make_async_copy(middle.at[place], target.at[place], sem.at[1, at, part]))
+    for copy in into:
+        copy.start()
+    for first, second in zip(into, out):
+        first.wait()
+        second.start()
+    for copy in out:
         copy.wait()
 
 
@@ -479,7 +495,7 @@
     hbm = pl.BlockSpec(memory_space=pl.ANY)
     semaphores = [
         (fronts // 2 + 1,), (5,), (LEVELS + 2,), (fronts // 2,), (fronts // 2,), (CUTS, count), (CUTS, count), (2,),
-        (devices,), (devices,), (LEVELS,), (LEVELS,),
+        (devices,), (devices,), (LEVELS, width // 128), (LEVELS, width // 128),
     ]
     results = pl.pallas_call(
         functools.partial(whole_kernel, fronts, leaves, capacity),
@@ -530,7 +546,8 @@
         out_shape=[jax.ShapeDtypeStruct(result.shape, result.dtype) for result in results],
         in_specs=[hbm] * 3,
         out_specs=[hbm] * 3,
-        scratch_shapes=[pltpu.SemaphoreType.DMA((3, SHARES))],
+        scratch_shapes=[pltpu.VMEM(result.shape, result.dtype) for result in results]
+        + [pltpu.SemaphoreType.DMA((2, 3, SHARES))],
         compiler_params=pltpu.CompilerParams(vmem_limit_bytes=62 * 2**20),
     )(*results)
     return (leaf_map[None], node_maps[None, None], top_rows[None, None])

time: 109 us -> 76.1 us (0.70)
  Pallas kernels: 107 us -> 74.7 us
    pallas_call x1, Pallas kernels: 33 us -> 2.14 us  [local(): pl.pallas_call(hand_on, out_shape=[jax.ShapeDtypeStruct(result.shape, res...]
    pallas_call x1, Pallas kernels: 74.1 us -> 72.5 us  [local(): pl.pallas_call(functools.partial(whole_kernel, fronts, leaves, capacity),...]
where the time goes in v5:
time: 76.1 us; the launch traced here: 75.9 us
  Pallas kernels  74.7 us (98%)
  between operations  1.29 us (2%)
    pallas_call x1, Pallas kernels, local(): pl.pallas_call(functools.partial(whole_kernel, fronts, leaves, capacity),...  72.5 us
    pallas_call x1, Pallas kernels, local(): pl.pallas_call(hand_on, out_shape=[jax.ShapeDtypeStruct(result.shape, res...  2.14 us

profile of v5, /device:TPU:0, one launch (start us, length us, event | category | flops | bytes accessed | tf_op | source)
XLA Modules:
  0.0 75.9 jit_solution(13337751574712944988)
XLA Ops:
  1.3 72.5 %shard_map.94 = (f32[1024,128]{1,0:T(8,128)}, f32[3,256,128]{2,1,0:T(8,128)}, f32[128,256]{1,0:T(8,128)}) custom-call(bf16[128,16384]{1,0:T(8,128)(2,1)} %c_ref.1, bf16[512,256]{1,0:T(8,128)(2,1)} %omega_ref.1, s32[32,128]{1,0:T(8,128)} %bitcast.7, s32[32,128]{1,0:T(8,128)} %bitcast.8, s32[1]{0:T(128)S(6)} %copy.10.size_hbm, s32[1,128]{1,0:T(1,128)} %bitcast.10, ...), custom_call_target="tpu_custom_call" | custom-call | flops 1073741824 | bytes 4194304 | tf_op jit(solution)/shard_map/pallas_call | solution.py:500
  73.8 2.1 %shard_map.95 = (f32[1024,128]{1,0:T(8,128)}, f32[3,256,128]{2,1,0:T(8,128)}, f32[128,256]{1,0:T(8,128)}) custom-call(f32[1024,128]{1,0:T(8,128)} %get-tuple-element.9.refs_0_, f32[3,256,128]{2,1,0:T(8,128)} %get-tuple-element.10.refs_1_, f32[128,256]{1,0:T(8,128)} %get-tuple-element.11.refs_2_), custom_call_target="tpu_custom_call" | custom-call | tf_op jit(solution)/shard_map/pallas_call | solution.py:544

commit v6 on v5

--- a/solution.py
+++ b/solution.py
@@ -39,8 +39,17 @@
     orders = (grp[:1] + xs + grp[1:], grp[:1] + near + grp[1 : len(grp) - half] + xs)
     link = {d: "x" if d in xs else "near" if d in near else "far" for d in grp + xs}
     free = {}
-    events = [(0.0, part, 0) for part in range(cuts)]
-    sequence = []
+    events = []
+    sequence = [(part, 0, orders[part % 2]) for part in range(cuts)]
+
+    def send(now, part, slot, dim):
+        begin = max(now, free.get(link[dim], 0.0))
+        free[link[dim]] = begin + 1.0
+        heapq.heappush(events, (begin + 1.0 + 0.2 * cuts, part, slot ^ dim))
+
+    for place in range(grp_bits + x_bits):
+        for part in range(cuts):
+            send(0.0, part, 0, orders[part % 2][place])
     while events:
         now, part, slot = heapq.heappop(events)
         order = orders[part % 2]
@@ -48,9 +57,7 @@
         onward = order[last + 1 :]
         sequence.append((part, slot, onward))
         for dim in onward:
-            begin = max(now, free.get(link[dim], 0.0))
-            free[link[dim]] = begin + 1.0
-            heapq.heappush(events, (begin + 1.0 + 0.2 * cuts, part, slot ^ dim))
+            send(now, part, slot, dim)
     return sequence
 
 
@@ -171,10 +178,9 @@
     sequence = exchange_plan(grp_bits, x_bits, CUTS)
     arrivals = {}
     given = []
-    for part, slot, onward in sequence:
-        if slot == 0:
-            for dim in onward:
-                arrivals[part, dim] = start(part, slot, dim)
+    for place in range(grp_bits + x_bits):
+        for part, slot, onward in sequence[:CUTS]:
+            arrivals[part, onward[place]] = start(part, slot, onward[place])
     for x in range(x_count):
         begin = pl.multiple_of((x * 2 + 1 - core) * span, 128)
         copy = pltpu.make_async_remote_copy(
@@ -292,11 +298,8 @@
             device_id_type=MESH,
         )
 
-    def deliver_start(step, carry):
+    for step in range(1, devices):
         deliver(step).start()
-        return carry
-
-    lax.fori_loop(1, devices, deliver_start, 0)
     arrived[pl.ds(myself, 1)] = packed[pl.ds(myself, 1)]
 
     def deliver_end(step, carry):
@@ -359,9 +362,10 @@
         gram = lax.dot_general(
             basis, basis, (((1,), (1,)), ((), ())), precision=HIGHEST, preferred_element_type=jnp.float32
         )
-        shift = 0.1 * (jnp.sum(gram * ident, keepdims=True) / rank) + 1e-05
+        trace = jnp.sum(gram * ident, keepdims=True)
+        shift = 0.1 * (trace / rank) + 1e-05
         gram = gram + shift * ident
-        scale = 1.0 / jnp.sum(gram * ident, keepdims=True)
+        scale = 1.0 / (trace + rank * shift)
         grams[at] = gram
         rest = ident - gram * scale
         state[at, pl.ds(0, rank), :] = (ident + rest) * scale

time: 76.1 us -> 78.2 us (1.028)
  Pallas kernels: 74.7 us -> 76.8 us
    pallas_call x1, Pallas kernels: 72.5 us -> 74.6 us  [local(): pl.pallas_call(functools.partial(whole_kernel, fronts, leaves, capacity),...]
where the time goes in v6:
time: 78.2 us; the launch traced here: 78.1 us
  Pallas kernels  76.8 us (98%)
  between operations  1.29 us (2%)
    pallas_call x1, Pallas kernels, local(): pl.pallas_call(functools.partial(whole_kernel, fronts, leaves, capacity),...  74.6 us
    pallas_call x1, Pallas kernels, local(): pl.pallas_call(hand_on, out_shape=[jax.ShapeDtypeStruct(result.shape, res...  2.14 us

profile of v6, /device:TPU:0, one launch (start us, length us, event | category | flops | bytes accessed | tf_op | source)
XLA Modules:
  0.0 78.1 jit_solution(9647125209701076041)
XLA Ops:
  1.3 74.6 %shard_map.94 = (f32[1024,128]{1,0:T(8,128)}, f32[3,256,128]{2,1,0:T(8,128)}, f32[128,256]{1,0:T(8,128)}) custom-call(bf16[128,16384]{1,0:T(8,128)(2,1)} %c_ref.1, bf16[512,256]{1,0:T(8,128)(2,1)} %omega_ref.1, s32[32,128]{1,0:T(8,128)} %bitcast.7, s32[32,128]{1,0:T(8,128)} %bitcast.8, s32[1]{0:T(128)S(6)} %copy.10.size_hbm, s32[1,128]{1,0:T(1,128)} %bitcast.10, ...), custom_call_target="tpu_custom_call" | custom-call | flops 1073741824 | bytes 4194304 | tf_op jit(solution)/shard_map/pallas_call | solution.py:504
  75.9 2.1 %shard_map.95 = (f32[1024,128]{1,0:T(8,128)}, f32[3,256,128]{2,1,0:T(8,128)}, f32[128,256]{1,0:T(8,128)}) custom-call(f32[1024,128]{1,0:T(8,128)} %get-tuple-element.9.refs_0_, f32[3,256,128]{2,1,0:T(8,128)} %get-tuple-element.10.refs_1_, f32[128,256]{1,0:T(8,128)} %get-tuple-element.11.refs_2_), custom_call_target="tpu_custom_call" | custom-call | tf_op jit(solution)/shard_map/pallas_call | solution.py:548

commit v7 on v6

--- a/solution.py
+++ b/solution.py
@@ -201,21 +201,25 @@
     lines = packed.shape[1]
     kept = capacity if capacity % 8 == 0 else lines
 
+    shape = (devices, lines, rows)
+    block_at = lax.broadcasted_iota(jnp.int32, shape, 0).astype(jnp.float32)
+    line_at = lax.broadcasted_iota(jnp.int32, shape, 1)
+    slot_at = jnp.where(line_at < used, lax.rem(line_at, capacity), -1).astype(jnp.float32)
+    row = lax.broadcasted_iota(jnp.int32, (rows, rows), 0)
+    col = lax.broadcasted_iota(jnp.int32, (rows, rows), 1)
+
     def make_tables():
         for copy in tables:
             copy.wait()
-        shape = (devices, lines, rows)
-        block_at = lax.broadcasted_iota(jnp.int32, shape, 0).astype(jnp.float32)
-        line_at = lax.broadcasted_iota(jnp.int32, shape, 1)
-        slot_at = jnp.where(line_at < used, lax.rem(line_at, capacity), -1).astype(jnp.float32)
-        row = lax.broadcasted_iota(jnp.int32, (rows, rows), 0)
-        col = lax.broadcasted_iota(jnp.int32, (rows, rows), 1)
         going = dest_ref[pl.ds(myself, 1), :].astype(jnp.float32)
         same = (column_of(going)[:, :rows] == going) & (row < col)
         rank_in = jnp.sum(same.astype(jnp.float32), axis=0, keepdims=True)
         placing = as_bf16((block_at == going.reshape(1, 1, rows)) & (slot_at == rank_in.reshape(1, 1, rows)))
         placing = placing.reshape(devices * lines, rows)
 
+        return placing
+
+    def make_landing():
         coming = dest_ref[...] == myself
         ahead = jnp.dot(as_bf16(coming), as_bf16(row < col), preferred_element_type=jnp.float32)
         ahead = jnp.where(coming, ahead, -2.0)
@@ -225,6 +229,9 @@
         where_to = jnp.sum(jnp.where(hit, landing.reshape(devices, 1, rows), 0.0), axis=2, keepdims=True) - 1.0
         where_to = where_to.reshape(devices * kept, 1)
         where_to = jnp.transpose(jnp.broadcast_to(where_to, (devices * kept, 128)))[0:1, :]
+        return where_to
+
+    def make_picks(where_to):
         chosen = as_bf16(column_of(leafskel_ref[...])[:, 0:1] == where_to)
         picks = []
         for level in range(LEVELS):
@@ -232,7 +239,7 @@
             wanted = column_of(mergeskel_ref[node])[:, 0:1]
             at = lax.broadcasted_iota(jnp.int32, (rank, 2 * rank), 1).astype(jnp.float32)
             picks.append(as_bf16(wanted == at))
-        return placing, where_to, chosen, picks
+        return chosen, picks
 
     def multiply(slot):
         x_from = flip(x_at, slot // leaves)
@@ -242,7 +249,6 @@
         acc[...] += jnp.dot(left, slots[slot], preferred_element_type=jnp.float32)
 
     held = {}
-    forwards = max(at for at, item in enumerate(sequence) if item[2])
     ready = False
     waiting = []
     for number, (part, slot, onward) in enumerate(sequence):
@@ -262,8 +268,12 @@
                 ready = True
             if waiting:
                 multiply(waiting.pop(0))
-        if number == forwards:
-            placing, where_to, chosen, picks = make_tables()
+        if number == len(sequence) // 2:
+            placing = make_tables()
+        if number == len(sequence) * 5 // 8:
+            where_to = make_landing()
+        if number == len(sequence) * 3 // 4:
+            chosen, picks = make_picks(where_to)
     for item in waiting:
         multiply(item)
 

time: 78.2 us -> 78.2 us (level)
  no operation moved by 1% of the time
where the time goes in v7:
time: 78.2 us; the launch traced here: 78.1 us
  Pallas kernels  76.8 us (98%)
  between operations  1.29 us (2%)
    pallas_call x1, Pallas kernels, local(): pl.pallas_call(functools.partial(whole_kernel, fronts, leaves, capacity),...  74.6 us
    pallas_call x1, Pallas kernels, local(): pl.pallas_call(hand_on, out_shape=[jax.ShapeDtypeStruct(result.shape, res...  2.14 us

profile of v7, /device:TPU:0, one launch (start us, length us, event | category | flops | bytes accessed | tf_op | source)
XLA Modules:
  0.0 78.1 jit_solution(11785442208956451676)
XLA Ops:
  1.3 74.6 %shard_map.94 = (f32[1024,128]{1,0:T(8,128)}, f32[3,256,128]{2,1,0:T(8,128)}, f32[128,256]{1,0:T(8,128)}) custom-call(bf16[128,16384]{1,0:T(8,128)(2,1)} %c_ref.1, bf16[512,256]{1,0:T(8,128)(2,1)} %omega_ref.1, s32[32,128]{1,0:T(8,128)} %bitcast.7, s32[32,128]{1,0:T(8,128)} %bitcast.8, s32[1]{0:T(128)S(6)} %copy.10.size_hbm, s32[1,128]{1,0:T(1,128)} %bitcast.10, ...), custom_call_target="tpu_custom_call" | custom-call | flops 1073741824 | bytes 4194304 | tf_op jit(solution)/shard_map/pallas_call | solution.py:514
  75.9 2.1 %shard_map.95 = (f32[1024,128]{1,0:T(8,128)}, f32[3,256,128]{2,1,0:T(8,128)}, f32[128,256]{1,0:T(8,128)}) custom-call(f32[1024,128]{1,0:T(8,128)} %get-tuple-element.9.refs_0_, f32[3,256,128]{2,1,0:T(8,128)} %get-tuple-element.10.refs_1_, f32[128,256]{1,0:T(8,128)} %get-tuple-element.11.refs_2_), custom_call_target="tpu_custom_call" | custom-call | tf_op jit(solution)/shard_map/pallas_call | solution.py:558
